TPU v7x, 32 devices: a whole 2x2x4 slice. The times are simulated.
32 devices in a mesh: groups: 2 (over y), ent: 16 (over z, x, core).
Axes of the slice: x: 2, y: 2, z: 4, core: 2. Of those that a mesh axis runs over, the one named last changes fastest.
Arguments:
- counts: int32 [32], P(('groups', 'ent')), parts along dimension 0, may hold values from 1 to 12, 96 in all
- src_index: int32 [384, 256], P(('groups', 'ent')), parts along dimension 0, may hold values from 0 to 1023
- dst_index: int32 [384, 256], P(('groups', 'ent')), parts along dimension 0, may hold values from 0 to 1023
- rel_index: int32 [384, 256], P(('groups', 'ent')), parts along dimension 0, may hold values from 0 to 4095
- neg_index: int32 [384, 512], P(('groups', 'ent')), parts along dimension 0, may hold values from 0 to 1023
- entity_table: bfloat16 [32768, 512], P(('groups', 'ent')), parts along dimension 0, may hold values from -1.1953125 to 1.1953125
- relation_table: float32 [4096, 512], replicated, may hold values from -6 to 6
Outputs:
- grad_table: float32 [32768, 512], P(('groups', 'ent')), parts along dimension 0
- grad_relation: float32 [8192, 512], P(('groups', 'ent')), parts along dimension 0
There are 2 independent parts, one for each index of `groups`. A program takes and returns all parts, laid end to end along the dimension named above; an argument that names none is the same for every part. Nothing has to cross between parts.
Inputs may be any that keep to these rules, and one draw needn't show every extreme that they name: The counts sum to 96, and the largest equals 12.
All inputs are finite; a program needn't handle non-finite values. No bound on the sum of `counts` on one device may be relied on, other than what follows from the above.
Results may differ from a plain program's by a relative error of at most 0.0029.
Values may be sent and summed in bfloat16 or wider, within the bound.
No kernel may reach another device: no remote copies, remote signals or barrier semaphores. Data moves between devices by JAX's collectives and lax.ppermute only.
A program may use at most 64 MiB of HBM per device.

v0:
```python
import functools

import jax
import jax.numpy as jnp
from jax import lax
from jax.experimental import pallas as pl
from jax.experimental.pallas import tpu as pltpu
from jax.sharding import PartitionSpec as P

margin = 0.1
BF = jnp.bfloat16
F32 = jnp.float32
BATCH = 16
LANES = 128
CHUNKS = 2

VMEM = pl.BlockSpec(memory_space=pltpu.VMEM)
SMEM = pl.BlockSpec(memory_space=pltpu.SMEM)
ANY = pl.BlockSpec(memory_space=pl.ANY)
HBM = pl.BlockSpec(memory_space=pltpu.HBM)


def list_row(info_ref, j, cap):
    pos = 2 * j + info_ref[2]
    second = pos >= info_ref[0]
    row = jnp.where(second, cap + pos - info_ref[0], pos)
    return row, second.astype(jnp.int32)


def span_count(info_ref):
    return (info_ref[0] + info_ref[1] + 1 - info_ref[2]) // 2


def pick_column(block, row):
    lane = lax.broadcasted_iota(jnp.int32, block.shape, 1)
    return jnp.sum(jnp.where(lane == row, block, 0), axis=1, keepdims=True)


def pack_kernel(counts_ref, *refs):
    arrays, out_ref, held, sems = refs[:4], refs[4], refs[5:9], refs[9]
    copies = [pltpu.make_async_copy(arrays[i], held[i], sems.at[i]) for i in range(4)]
    for copy in copies:
        copy.start()
    cap, length = arrays[0].shape[0], out_ref.shape[1]
    out_ref[...] = jnp.full(out_ref.shape, counts_ref[0], jnp.int32)
    at = 0
    for copy, ref in zip(copies, held):
        copy.wait()
        out_ref[:cap, at : at + ref.shape[1]] = ref[...]
        at += ref.shape[1]


def relay_kernel(x_ref, dep_ref, out_ref, sem):
    copy = pltpu.make_async_copy(x_ref, out_ref, sem)
    copy.start()
    copy.wait()


def prep_kernel(cap, info_ref, rel_ids_ref, ids_t_ref, table_ref, rows_ref, mult_ref):
    edges = rel_ids_ref.shape[1]
    ents = mult_ref.shape[2]

    def span(j, carry):
        row, _ = list_row(info_ref, j, cap)
        for e in range(edges):
            rows_ref[j, pl.ds(e, 1), :] = table_ref[pl.ds(rel_ids_ref[row, e], 1), :]
        total = jnp.zeros((8, ents), F32)
        neg = pick_column(ids_t_ref[3 * edges :, :], row)
        lane = lax.broadcasted_iota(jnp.int32, (8, ents), 1)
        for k in range(neg.shape[0] // 8):
            total = total + jnp.where(lane == neg[8 * k : 8 * k + 8], 1.0, 0.0)
        mult_ref[j] = jnp.sum(total, axis=0, keepdims=True)
        return carry

    lax.fori_loop(0, span_count(info_ref), span, 0)


def span_kernel(
    cap, info_ref, rel_ids_ref, ids_t_ref, ids_ref, rel_rows_ref, mult_ref,
    table_ref, far_ref, mate_table_ref, mate_far_ref,
    mixed_ref, scaled_ref, near_ref, *rest,
):
    keep_refs, give_refs = rest[:CHUNKS], rest[CHUNKS : 2 * CHUNKS]
    table, rel_acc, flat, rows, row_sems, table_sems = rest[2 * CHUNKS :]
    edges = rel_ids_ref.shape[1]
    ents = table_ref.shape[0]
    count = span_count(info_ref)

    @pl.when(info_ref[2] == 0)
    def _():
        pltpu.make_async_copy(table_ref, table.at[0], table_sems.at[0]).start()
        pltpu.make_async_copy(far_ref, table.at[1], table_sems.at[1]).start()

    @pl.when(info_ref[2] != 0)
    def _():
        pltpu.make_async_copy(mate_table_ref, table.at[0], table_sems.at[0]).start()
        pltpu.make_async_copy(mate_far_ref, table.at[1], table_sems.at[1]).start()

    def clear(i, c):
        rel_acc[pl.ds(i * 64, 64)] = jnp.zeros((64, *rel_acc.shape[1:]), F32)
        return c

    lax.fori_loop(0, rel_acc.shape[0] // 64, clear, 0)
    flat[...] = jnp.zeros(flat.shape, F32)
    pltpu.make_async_copy(table_ref, table.at[0], table_sems.at[0]).wait()
    pltpu.make_async_copy(far_ref, table.at[1], table_sems.at[1]).wait()

    def add_rows(row):
        for b in range(edges // BATCH):
            where_to = [rel_ids_ref[row, b * BATCH + i] for i in range(BATCH)]
            sums = [rel_acc[where_to[i]] + flat[b * BATCH + i] for i in range(BATCH)]
            for i in range(BATCH):
                rel_acc[where_to[i]] = sums[i]

    def fetch(j):
        slot = lax.rem(j, 2)
        return pltpu.make_async_copy(rel_rows_ref.at[j], rows.at[slot], row_sems.at[slot])

    @pl.when(count > 0)
    def _():
        fetch(0).start()

    e0 = lax.broadcasted_iota(jnp.int32, (edges, edges), 0) // BATCH
    e1 = lax.broadcasted_iota(jnp.int32, (edges, edges), 1) // BATCH

    def span(j, carry):
        fetch(j).wait()

        @pl.when(j + 1 < count)
        def _():
            fetch(j + 1).start()

        add_rows(list_row(info_ref, jnp.maximum(j - 1, 0), cap)[0])
        row, way = list_row(info_ref, j, cap)
        src = pick_column(ids_t_ref[0:edges, :], row)
        dst = pick_column(ids_t_ref[edges : 2 * edges, :], row)
        rel = pick_column(ids_t_ref[2 * edges : 3 * edges, :], row)
        rel_row = ids_ref[pl.ds(row, 1), 2 * edges : 3 * edges]
        lane = lax.broadcasted_iota(jnp.int32, (edges, ents), 1)
        far_table = table[1 - way]
        take = jnp.where(lane == src, 1.0, 0.0).astype(BF)
        source = jnp.dot(take, table[way], preferred_element_type=F32)
        rel_rows = rows[lax.rem(j, 2)]
        rotated = source * rel_rows
        score = lax.dot_general(
            rotated.astype(BF), far_table, (((1,), (1,)), ((), ())), preferred_element_type=F32
        )
        hit = lane == dst
        positive = jnp.sum(jnp.where(hit, score, 0.0), axis=1, keepdims=True)
        weights = mult_ref[j] / (1.0 + jnp.exp(positive - margin - score))
        totals = jnp.sum(weights, axis=1, keepdims=True)
        inverse = 1.0 / jnp.maximum(totals, 1e-30)
        mixed = (weights * inverse - jnp.where(hit, 1.0, 0.0)).astype(BF)
        mixed_ref[j] = mixed
        scaled_ref[j] = (rotated * totals).astype(BF)
        grad_rot = jnp.dot(mixed, far_table, preferred_element_type=F32) * totals
        near_ref[j] = (grad_rot * rel_rows).astype(BF)
        same = jnp.where((rel == rel_row) & (e0 == e1), 1.0, 0.0).astype(BF)
        grad_rel = grad_rot * source
        coarse = grad_rel.astype(BF)
        fine = (grad_rel - coarse.astype(F32)).astype(BF)
        summed = jnp.dot(same, coarse, preferred_element_type=F32) + jnp.dot(
            same, fine, preferred_element_type=F32
        )
        for q in range(flat.shape[1]):
            flat[:, q, :] = summed[:, q * LANES : (q + 1) * LANES]
        return carry

    lax.fori_loop(0, count, span, 0)

    @pl.when(count > 0)
    def _():
        add_rows(list_row(info_ref, jnp.maximum(count - 1, 0), cap)[0])

    pairs, part = keep_refs[0].shape[0], keep_refs[0].shape[1] // flat.shape[1]
    core = info_ref[3]

    def hand_out(c, carry):
        for h in range(CHUNKS):
            mine = (2 * c + core) * CHUNKS * part + h * part
            theirs = (2 * c + 1 - core) * CHUNKS * part + h * part
            keep_refs[h][c] = rel_acc[pl.ds(mine, part)].reshape(keep_refs[h].shape[1:])
            give_refs[h][c] = rel_acc[pl.ds(theirs, part)].reshape(keep_refs[h].shape[1:]).astype(BF)
        return carry

    lax.fori_loop(0, pairs, hand_out, 0)


def table_kernel(cap, side, info_ref, ids_ref, mixed_ref, scaled_ref, near_ref, dep_ref, acc_ref):
    edges, ents = near_ref.shape[1], acc_ref.shape[0]
    acc_ref[...] = jnp.zeros(acc_ref.shape, F32)

    def span(j, carry):
        row, way = list_row(info_ref, j, cap)

        @pl.when(way != side)
        def _():
            acc_ref[...] += lax.dot_general(
                mixed_ref[j], scaled_ref[j], (((0,), (0,)), ((), ())), preferred_element_type=F32
            )

        @pl.when(way == side)
        def _():
            level = lax.broadcasted_iota(jnp.int32, (ents, edges), 0)
            put = jnp.where(level == ids_ref[pl.ds(row, 1), 0:edges], 1.0, 0.0).astype(BF)
            acc_ref[...] += jnp.dot(put, near_ref[j], preferred_element_type=F32)

        return carry

    lax.fori_loop(0, span_count(info_ref), span, 0)


def fold_kernel(stage, info_ref, got_ref, keep_ref, dep_ref, give_out, keep_out):
    bit = info_ref[stage]
    for i in range(give_out.shape[0]):
        give, stay = 2 * i + 1 - bit, 2 * i + bit
        give_out[i] = (got_ref[give].astype(F32) + keep_ref[give]).astype(BF)
        keep_out[i] = got_ref[stay].astype(F32) + keep_ref[stay]


def far_kernel(info_ref, acc_ref, got_ref, dep_ref, out_ref):
    @pl.when(info_ref[2] == 0)
    def _():
        out_ref[...] = (acc_ref[...] + got_ref[...]).astype(BF)


def grad_table_kernel(info_ref, acc_ref, near_ref, back_ref, dep_ref, out_ref):
    @pl.when(info_ref[2] == 0)
    def _():
        out_ref[...] = acc_ref[...] + near_ref[...]

    @pl.when(info_ref[2] != 0)
    def _():
        out_ref[...] = back_ref[...].astype(F32)


def grad_relation_kernel(*refs):
    out_ref, total = refs[-2:]
    pieces = out_ref.shape[1] // LANES
    part = out_ref.shape[0] // CHUNKS
    for h in range(CHUNKS):
        total[...] = refs[h][0].astype(F32) + refs[CHUNKS + h][0]
        for q in range(pieces):
            out_ref[h * part : (h + 1) * part, q * LANES : (q + 1) * LANES] = total[
                pl.ds(q, part, stride=pieces), :
            ]


def tie(x, dep):
    return pl.pallas_call(
        lambda x_ref, dep_ref, out_ref: None,
        out_shape=jax.ShapeDtypeStruct(x.shape, x.dtype),
        in_specs=[ANY, ANY],
        out_specs=ANY,
        input_output_aliases={0: 0},
        name="tie",
    )(x, dep)


def params(mib):
    return pltpu.CompilerParams(vmem_limit_bytes=mib << 20)


def shards(counts, src_index, dst_index, rel_index, neg_index, entity_table, relation_table):
    devices = lax.axis_size("ent")
    half = devices // 2
    cap, edges = src_index.shape
    ents, width = entity_table.shape
    rels = relation_table.shape[0]
    pieces = width // LANES
    shape = jax.ShapeDtypeStruct
    me = lax.axis_index("ent")
    leads = [i for i in range(half) if i % 2 == 0] + [i for i in range(half, devices) if i % 2 == 1]
    lead = (me % 2) == (me // half)

    cross = [((i + half) % devices, i) for i in leads]
    back = [(i, (i + half) % devices) for i in leads]
    to_mate = [(i, i ^ 1) for i in leads]
    from_mate = [(i ^ 1, i) for i in leads]

    step = -(-(cap + 1) // 8) * 8
    index_arrays = (src_index, dst_index, rel_index, neg_index)
    mine = pl.pallas_call(
        pack_kernel,
        out_shape=shape((step, sum(a.shape[1] for a in index_arrays)), jnp.int32),
        in_specs=[SMEM] + [ANY] * 4,
        out_specs=VMEM,
        scratch_shapes=[pltpu.VMEM(a.shape, jnp.int32) for a in index_arrays] + [pltpu.SemaphoreType.DMA((4,))],
        compiler_params=params(2),
        name="pack",
    )(counts, *index_arrays)
    cross_mate = [(a, b ^ 1) for a, b in cross]
    from_lead = lax.ppermute(mine, "ent", to_mate)
    first = jnp.where(lead, mine, from_lead)
    second = lax.ppermute(mine, "ent", cross) + lax.ppermute(mine, "ent", cross_mate)
    sent = pl.pallas_call(
        relay_kernel,
        out_shape=shape(entity_table.shape, BF),
        in_specs=[ANY, ANY],
        out_specs=VMEM,
        scratch_shapes=[pltpu.SemaphoreType.DMA],
        compiler_params=params(2),
        name="relay",
    )(entity_table, second)
    far = lax.ppermute(sent, "ent", cross)
    ids = jnp.concatenate([first[:cap], second[:cap]], axis=0)
    bits = [(me >> b) & 1 for b in range(devices.bit_length() - 1)]
    info = jnp.stack([first[cap, 0], second[cap, 0], jnp.where(lead, 0, 1), *bits]).astype(jnp.int32)
    ids_t = ids.T
    rel_ids = ids[:, 2 * edges : 3 * edges]

    rel_rows, mult = pl.pallas_call(
        functools.partial(prep_kernel, cap),
        out_shape=(shape((cap, edges, width), F32), shape((cap, 1, ents), F32)),
        in_specs=[SMEM, SMEM, VMEM, VMEM],
        out_specs=(VMEM, VMEM),
        compiler_params=params(8),
        cost_estimate=pl.CostEstimate(flops=1, bytes_accessed=1, transcendentals=0),
        name="prep",
    )(info, rel_ids, ids_t, relation_table)

    far = tie(far, mult)
    mate_table = lax.ppermute(entity_table, "ent", to_mate)
    mate_far = lax.ppermute(far, "ent", to_mate)

    block = (devices // 2, rels // devices // CHUNKS * pieces, LANES)
    mixed, scaled, near, *rest = pl.pallas_call(
        functools.partial(span_kernel, cap),
        out_shape=(
            shape((cap, edges, ents), BF),
            shape((cap, edges, width), BF),
            shape((cap, edges, width), BF),
            *[shape(block, F32)] * CHUNKS,
            *[shape(block, BF)] * CHUNKS,
        ),
        in_specs=[SMEM, SMEM, VMEM, VMEM, HBM, VMEM] + [ANY] * 4,
        out_specs=(VMEM,) * (3 + 2 * CHUNKS),
        scratch_shapes=[
            pltpu.VMEM((2, ents, width), BF),
            pltpu.VMEM((rels, pieces, LANES), F32),
            pltpu.VMEM((edges, pieces, LANES), F32),
            pltpu.VMEM((2, edges, width), F32),
            pltpu.SemaphoreType.DMA((2,)),
            pltpu.SemaphoreType.DMA((2,)),
        ],
        compiler_params=params(30),
        name="spans",
    )(info, rel_ids, ids_t, ids, rel_rows, mult, entity_table, far, mate_table, mate_far)
    keep, give = rest[:CHUNKS], rest[CHUNKS:]

    def table_side(side, dep):
        return pl.pallas_call(
            functools.partial(table_kernel, cap, side),
            out_shape=shape((ents, width), F32),
            in_specs=[SMEM] + [VMEM] * 4 + [ANY],
            out_specs=VMEM,
            compiler_params=params(8),
            cost_estimate=pl.CostEstimate(
                flops=2 * cap * edges * ents * width, bytes_accessed=12 << 20, transcendentals=0
            ),
            name="tables",
        )(info, ids, mixed, scaled, near, dep)

    far_acc = table_side(1, mixed)
    far_got = lax.ppermute(far_acc, "ent", from_mate)

    dep, near_acc, returned, bit = scaled, None, None, 1
    got = [lax.ppermute(g, "ent", [(i, i ^ bit) for i in range(devices)]) for g in give]
    while 2 * bit < devices:
        give = []
        for h in range(CHUNKS):
            half_block = (got[h].shape[0] // 2, *block[1:])
            g, keep[h] = pl.pallas_call(
                functools.partial(fold_kernel, 3 + bit.bit_length()),
                out_shape=(shape(half_block, BF), shape(half_block, F32)),
                in_specs=[SMEM, VMEM, VMEM, ANY],
                out_specs=(VMEM, VMEM),
                compiler_params=params(4),
                name="fold",
            )(info, got[h], keep[h], dep)
            dep = g
            give.append(g)
        if returned is None:
            far_sum = pl.pallas_call(
                far_kernel,
                out_shape=shape((ents, width), BF),
                in_specs=[SMEM, VMEM, VMEM, ANY],
                out_specs=VMEM,
                compiler_params=params(4),
                name="far_sum",
            )(info, far_acc, far_got, dep)
            returned = lax.ppermute(far_sum, "ent", back)
            dep = returned
        elif near_acc is None and 4 * bit >= devices:
            near_acc = table_side(0, give[0])
            near_got = lax.ppermute(near_acc, "ent", from_mate)
        bit *= 2
        got = [lax.ppermute(g, "ent", [(i, i ^ bit) for i in range(devices)]) for g in give]

    grad_table = pl.pallas_call(
        grad_table_kernel,
        out_shape=shape((ents, width), F32),
        in_specs=[SMEM, VMEM, VMEM, VMEM, ANY],
        out_specs=VMEM,
        compiler_params=params(4),
        name="grad_table",
    )(info, near_acc, near_got, returned, dep)
    grad_relation = pl.pallas_call(
        grad_relation_kernel,
        out_shape=shape((rels // devices, width), F32),
        in_specs=[VMEM] * (2 * CHUNKS),
        out_specs=VMEM,
        scratch_shapes=[pltpu.VMEM(block[1:], F32)],
        compiler_params=params(4),
        name="grad_relation",
    )(*got, *keep)
    return (grad_table, grad_relation)


def solution(mesh):
    in_specs = (
        P(("groups", "ent")),
        P(("groups", "ent"), None),
        P(("groups", "ent"), None),
        P(("groups", "ent"), None),
        P(("groups", "ent"), None),
        P(("groups", "ent"), None),
        P(),
    )
    out_specs = (P(("groups", "ent"), None), P(("groups", "ent"), None))
    return jax.shard_map(shards, mesh=mesh, in_specs=in_specs, out_specs=out_specs, check_vma=False)
```

profile of v0, /device:TPU:0, one launch (start us, length us, event | category | flops | bytes accessed | tf_op | source)
XLA Modules:
  0.0 160.7 jit_solution(4090736766038980654)
XLA Ops:
  1.3 0.7 copy-done.6
  2.0 0.7 copy-done.7
  2.8 0.7 copy-done.8
  3.5 0.7 copy-done.9
  4.3 0.7 collective-permute-start.2
  5.0 1.3 collective-permute-start.1
  6.3 9.1 %collective-permute-done.1 = s32[16,1280]{1,0:T(8,128)S(1)} collective-permute-done((s32[16,1280]{1,0:T(8,128)S(1)}, s32[16,1280]{1,0:T(8,128)S(1)}, u32[]{:S(2)}, u32[]{:S(2)}) %collective-permute-start.1) | collective-permute-done | bytes 81952 | tf_op jit(solution)/shard_map/ppermute | solution.py:295
  15.5 1.2 relay.1
  16.7 1.3 collective-permute-start.3
  18.0 3.0 %collective-permute-start = (s32[16,1280]{1,0:T(8,128)S(1)}, s32[16,1280]{1,0:T(8,128)S(1)}, u32[]{:S(2)}, u32[]{:S(2)}) collective-permute-start(s32[16,1280]{1,0:T(8,128)S(1)} %pack.1), channel_id=1, source_target_pairs={{0,1},{2,3},{4,5},{6,7},{9,8},{11,10},{13,12},{15,14},{16,17},{18,... | collective-permute-start | bytes 245768 | tf_op jit(solution)/shard_map/ppermute | solution.py:293
  21.0 2.3 %collective-permute-start.4 = (bf16[1024,512]{1,0:T(8,128)(2,1)}, bf16[1024,512]{1,0:T(8,128)(2,1)}, u32[]{:S(2)}, u32[]{:S(2)}) collective-permute-start(bf16[1024,512]{1,0:T(8,128)(2,1)} %table_ref.3), channel_id=1, source_target_pairs={{0,1},{2,3},{4,5},{6,7},{9,8},{11,10},{13,12},{15,14},{16,17},{18,... | collective-permute-start | bytes 3145736 | tf_op jit(solution)/shard_map/ppermute | solution.py:323
  24.6 1.4 stack.23.info_ref
  26.0 3.4 %copy-done = f32[4096,512]{1,0:T(8,128)S(1)} copy-done((f32[4096,512]{1,0:T(8,128)S(1)}, f32[4096,512]{1,0:T(8,128)}, u32[]{:S(2)}) %copy-start) | copy-done | bytes 8388632
  29.3 3.3 %prep.1 = (f32[12,256,512]{2,1,0:T(8,128)S(1)}, f32[12,1,1024]{2,1,0:T(1,128)S(1)}) custom-call(s32[7]{0:T(128)S(1)} %stack.23.info_ref, s32[24,256]{1,0:T(8,128)S(1)} %fusion.rel_ids_ref, s32[1280,24]{1,0:T(8,128)S(1)} %copy.11.ids_t_ref, f32[4096,512]{1,0:T(8,128)S(1)} %copy-done), custom_call_target="tpu_custom_call" | custom-call | flops 1 | bytes 1 | tf_op jit(solution)/shard_map/prep/pallas_call | solution.py:312
  32.7 2.6 %copy-done.1 = f32[12,256,512]{2,1,0:T(8,128)} copy-done((f32[12,256,512]{2,1,0:T(8,128)}, f32[12,256,512]{2,1,0:T(8,128)S(1)}, u32[]{:S(2)}) %copy-start.1) | copy-done | bytes 6291480
  35.3 0.6 copy-done.4
  35.9 9.2 %collective-permute-done.3.x_ref = bf16[1024,512]{1,0:T(8,128)(2,1)S(1)} collective-permute-done((bf16[1024,512]{1,0:T(8,128)(2,1)S(1)}, bf16[1024,512]{1,0:T(8,128)(2,1)S(1)}, u32[]{:S(2)}, u32[]{:S(2)}) %collective-permute-start.3) | collective-permute-done | bytes 1048608 | tf_op jit(solution)/shard_map/ppermute | solution.py:305
  45.1 1.0 copy-done.2
  46.1 1.3 collective-permute-start.5
  47.4 2.4 %collective-permute-done.5.mate_far_ref = bf16[1024,512]{1,0:T(8,128)(2,1)S(1)} collective-permute-done((bf16[1024,512]{1,0:T(8,128)(2,1)}, bf16[1024,512]{1,0:T(8,128)(2,1)S(1)}, u32[]{:S(2)}, u32[]{:S(2)}) %collective-permute-start.5) | collective-permute-done | bytes 1048608 | tf_op jit(solution)/shard_map/ppermute | solution.py:324
  49.8 1.2 copy-done.3
  51.1 14.3 %spans.1 = (bf16[12,256,1024]{2,1,0:T(8,128)(2,1)S(1)}, bf16[12,256,512]{2,1,0:T(8,128)(2,1)S(1)}, bf16[12,256,512]{2,1,0:T(8,128)(2,1)S(1)}, f32[8,512,128]{2,1...) custom-call(s32[7]{0:T(128)S(1)} %stack.23.info_ref, ...), custom_call_target="tpu_custom_call" | custom-call | tf_op jit(solution)/shard_map/spans/pallas_call | solution.py:327
  65.4 2.5 %tables.2.acc_ref = f32[1024,512]{1,0:T(8,128)S(1)} custom-call(s32[7]{0:T(128)S(1)} %stack.23.info_ref, s32[24,1280]{1,0:T(8,128)S(1)} %pad_add_fusion.ids_ref, bf16[12,256,1024]{2,1,0:T(8,128)(2,1)S(1)} %get-tuple-element.25.mixed_ref.dep_ref, bf16[12,256,512]{2,1,0:T(8,128)(2,1)S(1)} %get-tuple-element.26.dep_ref.scaled_ref, ...), custom_call_target="tpu_custom_call" | custom-call | flops 3221225472 | bytes 12582912 | tf_op jit(solution)/shard_map/tables/pallas_call | solution.py:352
  67.9 1.3 collective-permute-start.8
  69.2 1.3 collective-permute-start.6
  70.6 4.9 %collective-permute-done.6.got_ref = bf16[8,512,128]{2,1,0:T(8,128)(2,1)S(1)} collective-permute-done((bf16[8,512,128]{2,1,0:T(8,128)(2,1)S(1)}, bf16[8,512,128]{2,1,0:T(8,128)(2,1)S(1)}, u32[]{:S(2)}, u32[]{:S(2)}) %collective-permute-start.6) | collective-permute-done | bytes 1048608 | tf_op jit(solution)/shard_map/ppermute | solution.py:368
  75.5 0.7 fold.6
  76.2 0.8 collective-permute-done.9.got_ref
  77.0 0.7 fold.7
  77.7 0.9 far_sum.1
  78.6 25.8 %collective-permute-start.10 = (bf16[1024,512]{1,0:T(8,128)(2,1)S(1)}, bf16[1024,512]{1,0:T(8,128)(2,1)S(1)}, u32[]{:S(2)}, u32[]{:S(2)}) collective-permute-start(bf16[1024,512]{1,0:T(8,128)(2,1)S(1)} %far_sum.1), channel_id=1, source_target_pairs={{0,8},{2,10},{4,12},{6,14},{9,1},{11,3},{13,5},{15,7},{16,24},{18,... | collective-permute-start | bytes 3145736 | tf_op jit(solution)/shard_map/ppermute | solution.py:392
  104.5 2.0 %collective-permute-start.12 = (bf16[4,512,128]{2,1,0:T(8,128)(2,1)S(1)}, bf16[4,512,128]{2,1,0:T(8,128)(2,1)S(1)}, u32[]{:S(2)}, u32[]{:S(2)}) collective-permute-start(bf16[4,512,128]{2,1,0:T(8,128)(2,1)S(1)} %get-tuple-element.34.dep_ref), channel_id=1, source_target_pairs={{0,2},{1,3},{2,0},{3,1},{4,6},{5,7},{6,4},{7,5},{8,10},{9,11},{10,... | collective-permute-start | bytes 1572872 | tf_op jit(solution)/shard_map/ppermute | solution.py:398
  106.5 7.2 %collective-permute-done.7.got_ref = bf16[4,512,128]{2,1,0:T(8,128)(2,1)S(1)} collective-permute-done((bf16[4,512,128]{2,1,0:T(8,128)(2,1)S(1)}, bf16[4,512,128]{2,1,0:T(8,128)(2,1)S(1)}, u32[]{:S(2)}, u32[]{:S(2)}) %collective-permute-start.7) | collective-permute-done | bytes 524320 | tf_op jit(solution)/shard_map/ppermute | solution.py:398
  113.6 3.0 %collective-permute-done.10.dep_ref.back_ref = bf16[1024,512]{1,0:T(8,128)(2,1)S(1)} collective-permute-done((bf16[1024,512]{1,0:T(8,128)(2,1)S(1)}, bf16[1024,512]{1,0:T(8,128)(2,1)S(1)}, u32[]{:S(2)}, u32[]{:S(2)}) %collective-permute-start.10) | collective-permute-done | bytes 1048608 | tf_op jit(solution)/shard_map/ppermute | solution.py:392
  116.6 0.6 fold.8
  117.3 1.9 %collective-permute-done.12.got_ref = bf16[4,512,128]{2,1,0:T(8,128)(2,1)S(1)} collective-permute-done((bf16[4,512,128]{2,1,0:T(8,128)(2,1)S(1)}, bf16[4,512,128]{2,1,0:T(8,128)(2,1)S(1)}, u32[]{:S(2)}, u32[]{:S(2)}) %collective-permute-start.12) | collective-permute-done | bytes 524320 | tf_op jit(solution)/shard_map/ppermute | solution.py:398
  119.3 0.7 fold.9
  119.9 5.3 %collective-permute-done.11.got_ref = bf16[2,512,128]{2,1,0:T(8,128)(2,1)S(1)} collective-permute-done((bf16[2,512,128]{2,1,0:T(8,128)(2,1)S(1)}, bf16[2,512,128]{2,1,0:T(8,128)(2,1)S(1)}, u32[]{:S(2)}, u32[]{:S(2)}) %collective-permute-start.11) | collective-permute-done | bytes 262176 | tf_op jit(solution)/shard_map/ppermute | solution.py:398
  125.2 0.6 fold.10
  125.8 2.5 %tables.3.acc_ref = f32[1024,512]{1,0:T(8,128)S(1)} custom-call(s32[7]{0:T(128)S(1)} %stack.23.info_ref, s32[24,1280]{1,0:T(8,128)S(1)} %pad_add_fusion.ids_ref, bf16[12,256,1024]{2,1,0:T(8,128)(2,1)S(1)} %get-tuple-element.25.mixed_ref.dep_ref, bf16[12,256,512]{2,1,0:T(8,128)(2,1)S(1)} %get-tuple-element.26.dep_ref.scaled_ref, ...), custom_call_target="tpu_custom_call" | custom-call | flops 3221225472 | bytes 12582912 | tf_op jit(solution)/shard_map/tables/pallas_call | solution.py:352
  128.4 1.3 collective-permute-start.13
  129.7 0.8 collective-permute-start.14
  130.4 8.2 %collective-permute-done.14.got_ref = bf16[2,512,128]{2,1,0:T(8,128)(2,1)S(1)} collective-permute-done((bf16[2,512,128]{2,1,0:T(8,128)(2,1)S(1)}, bf16[2,512,128]{2,1,0:T(8,128)(2,1)S(1)}, u32[]{:S(2)}, u32[]{:S(2)}) %collective-permute-start.14) | collective-permute-done | bytes 262176 | tf_op jit(solution)/shard_map/ppermute | solution.py:398
  139.2 8.1 %collective-permute-start.16 = (bf16[1,512,128]{2,1,0:T(8,128)(2,1)S(1)}, bf16[1,512,128]{2,1,0:T(8,128)(2,1)S(1)}, u32[]{:S(2)}, u32[]{:S(2)}) collective-permute-start(bf16[1,512,128]{2,1,0:T(8,128)(2,1)S(1)} %get-tuple-element.41.dep_ref), channel_id=1, source_target_pairs={{0,8},{1,9},{2,10},{3,11},{4,12},{5,13},{6,14},{7,15},{8,0},{9,1},... | collective-permute-start | bytes 393224 | tf_op jit(solution)/shard_map/ppermute | solution.py:398
  147.4 8.4 %collective-permute-done.16.refs_1_ = bf16[1,512,128]{2,1,0:T(8,128)(2,1)S(1)} collective-permute-done((bf16[1,512,128]{2,1,0:T(8,128)(2,1)S(1)}, bf16[1,512,128]{2,1,0:T(8,128)(2,1)S(1)}, u32[]{:S(2)}, u32[]{:S(2)}) %collective-permute-start.16) | collective-permute-done | bytes 131104 | tf_op jit(solution)/shard_map/ppermute | solution.py:398
  155.7 2.0 %collective-permute-done.15.refs_0_ = bf16[1,512,128]{2,1,0:T(8,128)(2,1)S(1)} collective-permute-done((bf16[1,512,128]{2,1,0:T(8,128)(2,1)S(1)}, bf16[1,512,128]{2,1,0:T(8,128)(2,1)S(1)}, u32[]{:S(2)}, u32[]{:S(2)}) %collective-permute-start.15) | collective-permute-done | bytes 131104 | tf_op jit(solution)/shard_map/ppermute | solution.py:398
  157.7 0.9 grad_relation.1
  158.6 2.1 %grad_table.1 = f32[1024,512]{1,0:T(8,128)} custom-call(s32[7]{0:T(128)S(1)} %stack.23.info_ref, f32[1024,512]{1,0:T(8,128)S(1)} %tables.3.acc_ref, f32[1024,512]{1,0:T(8,128)S(1)} %collective-permute-done.13.near_ref, bf16[1024,512]{1,0:T(8,128)(2,1)S(1)} %collective-permute-done.10.dep_ref.back_ref, bf16[1,512,128]{2,1,0:T(8,128)(2,1)S(1)} %get-tuple-element.41.dep_ref), custom_call_target="tpu_custom_call" | custom-call | tf_op jit(solution)/shard_map/grad_table/pallas_call | solution.py:400
  (31 shorter events, 2.4 us)
Async XLA Ops:
  1.3 0.8 copy-start.6
  2.0 0.7 copy-start.7
  2.8 0.7 copy-start.8
  3.5 0.7 copy-start.9
  4.3 2.0 %collective-permute-start.2 = (s32[16,1280]{1,0:T(8,128)S(1)}, s32[16,1280]{1,0:T(8,128)S(1)}, u32[]{:S(2)}, u32[]{:S(2)}) collective-permute-start(s32[16,1280]{1,0:T(8,128)S(1)} %pack.1), channel_id=1, source_target_pairs={{8,1},{10,3},{12,5},{14,7},{1,8},{3,10},{5,12},{7,14},{24,17},{26,... | collective-permute-start | bytes 245768 | tf_op jit(solution)/shard_map/ppermute | solution.py:295
  5.0 10.5 %collective-permute-start.1 = (s32[16,1280]{1,0:T(8,128)S(1)}, s32[16,1280]{1,0:T(8,128)S(1)}, u32[]{:S(2)}, u32[]{:S(2)}) collective-permute-start(s32[16,1280]{1,0:T(8,128)S(1)} %pack.1), channel_id=1, source_target_pairs={{8,0},{10,2},{12,4},{14,6},{1,9},{3,11},{5,13},{7,15},{24,16},{26,... | collective-permute-start | bytes 245768 | tf_op jit(solution)/shard_map/ppermute | solution.py:295
  16.7 28.4 %collective-permute-start.3 = (bf16[1024,512]{1,0:T(8,128)(2,1)S(1)}, bf16[1024,512]{1,0:T(8,128)(2,1)S(1)}, u32[]{:S(2)}, u32[]{:S(2)}) collective-permute-start(bf16[1024,512]{1,0:T(8,128)(2,1)S(1)} %relay.1), channel_id=1, source_target_pairs={{8,0},{10,2},{12,4},{14,6},{1,9},{3,11},{5,13},{7,15},{24,16},{26,... | collective-permute-start | bytes 3145736 | tf_op jit(solution)/shard_map/ppermute | solution.py:305
  18.0 5.8 %collective-permute-start = (s32[16,1280]{1,0:T(8,128)S(1)}, s32[16,1280]{1,0:T(8,128)S(1)}, u32[]{:S(2)}, u32[]{:S(2)}) collective-permute-start(s32[16,1280]{1,0:T(8,128)S(1)} %pack.1), channel_id=1, source_target_pairs={{0,1},{2,3},{4,5},{6,7},{9,8},{11,10},{13,12},{15,14},{16,17},{18,... | collective-permute-start | bytes 245768 | tf_op jit(solution)/shard_map/ppermute | solution.py:293
  21.0 26.4 %collective-permute-start.4 = (bf16[1024,512]{1,0:T(8,128)(2,1)}, bf16[1024,512]{1,0:T(8,128)(2,1)}, u32[]{:S(2)}, u32[]{:S(2)}) collective-permute-start(bf16[1024,512]{1,0:T(8,128)(2,1)} %table_ref.3), channel_id=1, source_target_pairs={{0,1},{2,3},{4,5},{6,7},{9,8},{11,10},{13,12},{15,14},{16,17},{18,... | collective-permute-start | bytes 3145736 | tf_op jit(solution)/shard_map/ppermute | solution.py:323
  26.0 3.4 %copy-start = (f32[4096,512]{1,0:T(8,128)S(1)}, f32[4096,512]{1,0:T(8,128)}, u32[]{:S(2)}) copy-start(f32[4096,512]{1,0:T(8,128)} %table_ref.2) | copy-start | bytes 25165828
  32.7 2.6 %copy-start.1 = (f32[12,256,512]{2,1,0:T(8,128)}, f32[12,256,512]{2,1,0:T(8,128)S(1)}, u32[]{:S(2)}) copy-start(f32[12,256,512]{2,1,0:T(8,128)S(1)} %get-tuple-element.23.rel_rows_ref) | copy-start | bytes 18874372
  35.3 0.6 copy-start.4
  45.1 1.0 copy-start.2
  45.1 4.7 %copy-start.5 = (f32[12,1,1024]{2,1,0:T(1,128)S(1)}, f32[12,1,1024]{2,1,0:T(1,128)}, u32[]{:S(2)}) copy-start(f32[12,1,1024]{2,1,0:T(1,128)} %copy-done.4) | copy-start | bytes 147460
  46.1 3.8 %collective-permute-start.5 = (bf16[1024,512]{1,0:T(8,128)(2,1)}, bf16[1024,512]{1,0:T(8,128)(2,1)S(1)}, u32[]{:S(2)}, u32[]{:S(2)}) collective-permute-start(bf16[1024,512]{1,0:T(8,128)(2,1)} %tie.1.far_ref), channel_id=1, source_target_pairs={{0,1},{2,3},{4,5},{6,7},{9,8},{11,10},{13,12},{15,14},{16,17},{18,... | collective-permute-start | bytes 3145736 | tf_op jit(solution)/shard_map/ppermute | solution.py:324
  49.8 1.2 copy-start.3
  67.9 9.8 %collective-permute-start.8 = (f32[1024,512]{1,0:T(8,128)S(1)}, f32[1024,512]{1,0:T(8,128)S(1)}, u32[]{:S(2)}, u32[]{:S(2)}) collective-permute-start(f32[1024,512]{1,0:T(8,128)S(1)} %tables.2.acc_ref), channel_id=1, source_target_pairs={{1,0},{3,2},{5,4},{7,6},{8,9},{10,11},{12,13},{14,15},{17,16},{19,... | collective-permute-start | bytes 6291464 | tf_op jit(solution)/shard_map/ppermute | solution.py:365
  69.2 6.3 %collective-permute-start.6 = (bf16[8,512,128]{2,1,0:T(8,128)(2,1)S(1)}, bf16[8,512,128]{2,1,0:T(8,128)(2,1)S(1)}, u32[]{:S(2)}, u32[]{:S(2)}) collective-permute-start(bf16[8,512,128]{2,1,0:T(8,128)(2,1)S(1)} %get-tuple-element.28), channel_id=1, source_target_pairs={{0,1},{1,0},{2,3},{3,2},{4,5},{5,4},{6,7},{7,6},{8,9},{9,8},{10,11... | collective-permute-start | bytes 3145736 | tf_op jit(solution)/shard_map/ppermute | solution.py:368
  70.5 6.4 %collective-permute-start.9 = (bf16[8,512,128]{2,1,0:T(8,128)(2,1)S(1)}, bf16[8,512,128]{2,1,0:T(8,128)(2,1)S(1)}, u32[]{:S(2)}, u32[]{:S(2)}) collective-permute-start(bf16[8,512,128]{2,1,0:T(8,128)(2,1)S(1)} %get-tuple-element.32), channel_id=1, source_target_pairs={{0,1},{1,0},{2,3},{3,2},{4,5},{5,4},{6,7},{7,6},{8,9},{9,8},{10,11... | collective-permute-start | bytes 3145736 | tf_op jit(solution)/shard_map/ppermute | solution.py:368
  78.6 38.0 %collective-permute-start.10 = (bf16[1024,512]{1,0:T(8,128)(2,1)S(1)}, bf16[1024,512]{1,0:T(8,128)(2,1)S(1)}, u32[]{:S(2)}, u32[]{:S(2)}) collective-permute-start(bf16[1024,512]{1,0:T(8,128)(2,1)S(1)} %far_sum.1), channel_id=1, source_target_pairs={{0,8},{2,10},{4,12},{6,14},{9,1},{11,3},{13,5},{15,7},{16,24},{18,... | collective-permute-start | bytes 3145736 | tf_op jit(solution)/shard_map/ppermute | solution.py:392
  104.4 9.2 %collective-permute-start.7 = (bf16[4,512,128]{2,1,0:T(8,128)(2,1)S(1)}, bf16[4,512,128]{2,1,0:T(8,128)(2,1)S(1)}, u32[]{:S(2)}, u32[]{:S(2)}) collective-permute-start(bf16[4,512,128]{2,1,0:T(8,128)(2,1)S(1)} %get-tuple-element.30.dep_ref), channel_id=1, source_target_pairs={{0,2},{1,3},{2,0},{3,1},{4,6},{5,7},{6,4},{7,5},{8,10},{9,11},{10,... | collective-permute-start | bytes 1572872 | tf_op jit(solution)/shard_map/ppermute | solution.py:398
  104.5 14.8 %collective-permute-start.12 = (bf16[4,512,128]{2,1,0:T(8,128)(2,1)S(1)}, bf16[4,512,128]{2,1,0:T(8,128)(2,1)S(1)}, u32[]{:S(2)}, u32[]{:S(2)}) collective-permute-start(bf16[4,512,128]{2,1,0:T(8,128)(2,1)S(1)} %get-tuple-element.34.dep_ref), channel_id=1, source_target_pairs={{0,2},{1,3},{2,0},{3,1},{4,6},{5,7},{6,4},{7,5},{8,10},{9,11},{10,... | collective-permute-start | bytes 1572872 | tf_op jit(solution)/shard_map/ppermute | solution.py:398
  117.3 8.0 %collective-permute-start.11 = (bf16[2,512,128]{2,1,0:T(8,128)(2,1)S(1)}, bf16[2,512,128]{2,1,0:T(8,128)(2,1)S(1)}, u32[]{:S(2)}, u32[]{:S(2)}) collective-permute-start(bf16[2,512,128]{2,1,0:T(8,128)(2,1)S(1)} %get-tuple-element.35.dep_ref), channel_id=1, source_target_pairs={{0,4},{1,5},{2,6},{3,7},{4,0},{5,1},{6,2},{7,3},{8,12},{9,13},{10,... | collective-permute-start | bytes 786440 | tf_op jit(solution)/shard_map/ppermute | solution.py:398
  128.4 30.2 %collective-permute-start.13 = (f32[1024,512]{1,0:T(8,128)S(1)}, f32[1024,512]{1,0:T(8,128)S(1)}, u32[]{:S(2)}, u32[]{:S(2)}) collective-permute-start(f32[1024,512]{1,0:T(8,128)S(1)} %tables.3.acc_ref), channel_id=1, source_target_pairs={{1,0},{3,2},{5,4},{7,6},{8,9},{10,11},{12,13},{14,15},{17,16},{19,... | collective-permute-start | bytes 6291464 | tf_op jit(solution)/shard_map/ppermute | solution.py:396
  129.7 9.0 %collective-permute-start.14 = (bf16[2,512,128]{2,1,0:T(8,128)(2,1)S(1)}, bf16[2,512,128]{2,1,0:T(8,128)(2,1)S(1)}, u32[]{:S(2)}, u32[]{:S(2)}) collective-permute-start(bf16[2,512,128]{2,1,0:T(8,128)(2,1)S(1)} %get-tuple-element.38.dep_ref), channel_id=1, source_target_pairs={{0,4},{1,5},{2,6},{3,7},{4,0},{5,1},{6,2},{7,3},{8,12},{9,13},{10,... | collective-permute-start | bytes 786440 | tf_op jit(solution)/shard_map/ppermute | solution.py:398
  139.2 16.5 %collective-permute-start.16 = (bf16[1,512,128]{2,1,0:T(8,128)(2,1)S(1)}, bf16[1,512,128]{2,1,0:T(8,128)(2,1)S(1)}, u32[]{:S(2)}, u32[]{:S(2)}) collective-permute-start(bf16[1,512,128]{2,1,0:T(8,128)(2,1)S(1)} %get-tuple-element.41.dep_ref), channel_id=1, source_target_pairs={{0,8},{1,9},{2,10},{3,11},{4,12},{5,13},{6,14},{7,15},{8,0},{9,1},... | collective-permute-start | bytes 393224 | tf_op jit(solution)/shard_map/ppermute | solution.py:398
  147.3 10.4 %collective-permute-start.15 = (bf16[1,512,128]{2,1,0:T(8,128)(2,1)S(1)}, bf16[1,512,128]{2,1,0:T(8,128)(2,1)S(1)}, u32[]{:S(2)}, u32[]{:S(2)}) collective-permute-start(bf16[1,512,128]{2,1,0:T(8,128)(2,1)S(1)} %get-tuple-element.39.dep_ref), channel_id=1, source_target_pairs={{0,8},{1,9},{2,10},{3,11},{4,12},{5,13},{6,14},{7,15},{8,0},{9,1},... | collective-permute-start | bytes 393224 | tf_op jit(solution)/shard_map/ppermute | solution.py:398
where the time goes:
time: 160 us; the launch traced here: 161 us
  waiting for transfers between devices  62.2 us (39%)
  starting transfers between devices  50.7 us (32%)
  Pallas kernels  31.8 us (20%)
  local copies, waits for them, and re-layouts  14.3 us (9%)
    ppermute x8, waiting for transfers between devices, shards(): lax.ppermute(g, 'ent', [(i, i ^ bit) for i in range(devices)])  38.5 us
    ppermute x1, starting transfers between devices, shards(): returned = lax.ppermute(far_sum, 'ent', back)  25.8 us
    pallas_call x1, Pallas kernels, shards(): pl.pallas_call(functools.partial(span_kernel, cap), out_shape=(shape((cap...  14.3 us
    ppermute x8, starting transfers between devices, shards(): lax.ppermute(g, 'ent', [(i, i ^ bit) for i in range(devices)])  12.5 us
    unnamed x20, local copies, waits for them, and re-layouts  11.7 us
    ppermute x1, waiting for transfers between devices, shards(): far = lax.ppermute(sent, 'ent', cross)  9.16 us
    ppermute x1, waiting for transfers between devices, shards(): lax.ppermute(mine, 'ent', cross) + lax.ppermute(mine, 'ent', cross_mate)  9.14 us
    pallas_call x2, Pallas kernels, table_side(): pl.pallas_call(functools.partial(table_kernel, cap, side), out_shape=shap...  5.06 us
  transfers between devices with their start and end apart: 17, of which 12 were waited for; matrix products, arithmetic and copies ran while one was open for 2% of the time, Pallas kernels for 5%

commit v1 on v0

--- a/solution.py
+++ b/solution.py
@@ -364,7 +364,10 @@
     far_acc = table_side(1, mixed)
     far_got = lax.ppermute(far_acc, "ent", from_mate)
 
-    dep, near_acc, returned, bit = scaled, None, None, 1
+    near_acc = table_side(0, far_acc)
+    near_got = lax.ppermute(near_acc, "ent", from_mate)
+
+    dep, returned, bit = near_acc, None, 1
     got = [lax.ppermute(g, "ent", [(i, i ^ bit) for i in range(devices)]) for g in give]
     while 2 * bit < devices:
         give = []
@@ -391,9 +394,6 @@
             )(info, far_acc, far_got, dep)
             returned = lax.ppermute(far_sum, "ent", back)
             dep = returned
-        elif near_acc is None and 4 * bit >= devices:
-            near_acc = table_side(0, give[0])
-            near_got = lax.ppermute(near_acc, "ent", from_mate)
         bit *= 2
         got = [lax.ppermute(g, "ent", [(i, i ^ bit) for i in range(devices)]) for g in give]
 

time: 160 us -> 150 us (0.938)
  the two profiles are of different devices: /device:TPU:0 before, /device:TPU:4 now
where the time goes in v1:
time: 150 us; the launch traced here: 149 us
  waiting for transfers between devices  46.5 us (31%)
  Pallas kernels  44 us (29%)
  starting transfers between devices  42.9 us (29%)
  local copies, waits for them, and re-layouts  14.3 us (10%)
  between operations  1.53 us (1%)
    ppermute x8, waiting for transfers between devices, shards(): lax.ppermute(g, 'ent', [(i, i ^ bit) for i in range(devices)])  25.8 us
    pallas_call x1, Pallas kernels, shards(): pl.pallas_call(functools.partial(span_kernel, cap), out_shape=(shape((cap...  21.9 us
    ppermute x1, starting transfers between devices, shards(): returned = lax.ppermute(far_sum, 'ent', back)  19.8 us
    unnamed x20, local copies, waits for them, and re-layouts  11.7 us
    ppermute x8, starting transfers between devices, shards(): lax.ppermute(g, 'ent', [(i, i ^ bit) for i in range(devices)])  10.6 us
    pallas_call x2, Pallas kernels, table_side(): pl.pallas_call(functools.partial(table_kernel, cap, side), out_shape=shap...  7.81 us
    ppermute x1, waiting for transfers between devices, shards(): lax.ppermute(mine, 'ent', cross) + lax.ppermute(mine, 'ent', cross_mate)  7.69 us
    ppermute x1, waiting for transfers between devices, shards(): far = lax.ppermute(sent, 'ent', cross)  7.39 us
  transfers between devices with their start and end apart: 17, of which 11 were waited for; matrix products, arithmetic and copies ran while one was open for 2% of the time, Pallas kernels for 11%

profile of v1, /device:TPU:4, one launch (start us, length us, event | category | flops | bytes accessed | tf_op | source)
XLA Modules:
  0.0 149.3 jit_solution(2041319241563227823)
XLA Ops:
  1.3 0.7 copy-done.6
  2.0 0.7 copy-done.7
  2.8 0.7 copy-done.8
  3.5 0.7 copy-done.9
  4.3 0.7 collective-permute-start.2
  5.0 1.3 collective-permute-start.1
  6.3 7.7 %collective-permute-done.1 = s32[16,1280]{1,0:T(8,128)S(1)} collective-permute-done((s32[16,1280]{1,0:T(8,128)S(1)}, s32[16,1280]{1,0:T(8,128)S(1)}, u32[]{:S(2)}, u32[]{:S(2)}) %collective-permute-start.1) | collective-permute-done | bytes 81952 | tf_op jit(solution)/shard_map/ppermute | solution.py:295
  14.0 1.2 relay.1
  15.3 1.3 collective-permute-start.3
  16.6 3.0 %collective-permute-start = (s32[16,1280]{1,0:T(8,128)S(1)}, s32[16,1280]{1,0:T(8,128)S(1)}, u32[]{:S(2)}, u32[]{:S(2)}) collective-permute-start(s32[16,1280]{1,0:T(8,128)S(1)} %pack.1), channel_id=1, source_target_pairs={{0,1},{2,3},{4,5},{6,7},{9,8},{11,10},{13,12},{15,14},{16,17},{18,... | collective-permute-start | bytes 245768 | tf_op jit(solution)/shard_map/ppermute | solution.py:293
  19.6 2.3 %collective-permute-start.4 = (bf16[1024,512]{1,0:T(8,128)(2,1)}, bf16[1024,512]{1,0:T(8,128)(2,1)}, u32[]{:S(2)}, u32[]{:S(2)}) collective-permute-start(bf16[1024,512]{1,0:T(8,128)(2,1)} %table_ref.3), channel_id=1, source_target_pairs={{0,1},{2,3},{4,5},{6,7},{9,8},{11,10},{13,12},{15,14},{16,17},{18,... | collective-permute-start | bytes 3145736 | tf_op jit(solution)/shard_map/ppermute | solution.py:323
  21.8 0.5 slice.21
  22.4 0.5 slice.20
  23.1 1.4 stack.23.info_ref
  24.5 3.4 %copy-done = f32[4096,512]{1,0:T(8,128)S(1)} copy-done((f32[4096,512]{1,0:T(8,128)S(1)}, f32[4096,512]{1,0:T(8,128)}, u32[]{:S(2)}) %copy-start) | copy-done | bytes 8388632
  27.9 5.1 %prep.1 = (f32[12,256,512]{2,1,0:T(8,128)S(1)}, f32[12,1,1024]{2,1,0:T(1,128)S(1)}) custom-call(s32[7]{0:T(128)S(1)} %stack.23.info_ref, s32[24,256]{1,0:T(8,128)S(1)} %fusion.rel_ids_ref, s32[1280,24]{1,0:T(8,128)S(1)} %copy.11.ids_t_ref, f32[4096,512]{1,0:T(8,128)S(1)} %copy-done), custom_call_target="tpu_custom_call" | custom-call | flops 1 | bytes 1 | tf_op jit(solution)/shard_map/prep/pallas_call | solution.py:312
  33.0 2.6 %copy-done.1 = f32[12,256,512]{2,1,0:T(8,128)} copy-done((f32[12,256,512]{2,1,0:T(8,128)}, f32[12,256,512]{2,1,0:T(8,128)S(1)}, u32[]{:S(2)}) %copy-start.1) | copy-done | bytes 6291480
  35.6 0.6 copy-done.4
  36.3 7.4 %collective-permute-done.3.x_ref = bf16[1024,512]{1,0:T(8,128)(2,1)S(1)} collective-permute-done((bf16[1024,512]{1,0:T(8,128)(2,1)S(1)}, bf16[1024,512]{1,0:T(8,128)(2,1)S(1)}, u32[]{:S(2)}, u32[]{:S(2)}) %collective-permute-start.3) | collective-permute-done | bytes 1048608 | tf_op jit(solution)/shard_map/ppermute | solution.py:305
  43.6 1.0 copy-done.2
  44.6 1.3 collective-permute-start.5
  46.0 2.4 %collective-permute-done.5.mate_far_ref = bf16[1024,512]{1,0:T(8,128)(2,1)S(1)} collective-permute-done((bf16[1024,512]{1,0:T(8,128)(2,1)}, bf16[1024,512]{1,0:T(8,128)(2,1)S(1)}, u32[]{:S(2)}, u32[]{:S(2)}) %collective-permute-start.5) | collective-permute-done | bytes 1048608 | tf_op jit(solution)/shard_map/ppermute | solution.py:324
  48.4 1.2 copy-done.3
  49.6 21.9 %spans.1 = (bf16[12,256,1024]{2,1,0:T(8,128)(2,1)S(1)}, bf16[12,256,512]{2,1,0:T(8,128)(2,1)S(1)}, bf16[12,256,512]{2,1,0:T(8,128)(2,1)S(1)}, f32[8,512,128]{2,1...) custom-call(s32[7]{0:T(128)S(1)} %stack.23.info_ref, ...), custom_call_target="tpu_custom_call" | custom-call | tf_op jit(solution)/shard_map/spans/pallas_call | solution.py:327
  71.5 4.0 %tables.2.dep_ref.acc_ref = f32[1024,512]{1,0:T(8,128)S(1)} custom-call(s32[7]{0:T(128)S(1)} %stack.23.info_ref, s32[24,1280]{1,0:T(8,128)S(1)} %pad_add_fusion.ids_ref, bf16[12,256,1024]{2,1,0:T(8,128)(2,1)S(1)} %get-tuple-element.25.mixed_ref.dep_ref, bf16[12,256,512]{2,1,0:T(8,128)(2,1)S(1)} %get-tuple-element.26.scaled_ref, ...), custom_call_target="tpu_custom_call" | custom-call | flops 3221225472 | bytes 12582912 | tf_op jit(solution)/shard_map/tables/pallas_call | solution.py:352
  75.5 1.3 collective-permute-start.7
  76.8 1.3 collective-permute-start.9
  78.2 3.8 %tables.3.dep_ref.acc_ref = f32[1024,512]{1,0:T(8,128)S(1)} custom-call(s32[7]{0:T(128)S(1)} %stack.23.info_ref, s32[24,1280]{1,0:T(8,128)S(1)} %pad_add_fusion.ids_ref, bf16[12,256,1024]{2,1,0:T(8,128)(2,1)S(1)} %get-tuple-element.25.mixed_ref.dep_ref, bf16[12,256,512]{2,1,0:T(8,128)(2,1)S(1)} %get-tuple-element.26.scaled_ref, ...), custom_call_target="tpu_custom_call" | custom-call | flops 3221225472 | bytes 12582912 | tf_op jit(solution)/shard_map/tables/pallas_call | solution.py:352
  82.0 1.3 collective-permute-start.6
  83.3 0.7 fold.6
  84.5 0.7 fold.7
  85.3 0.9 far_sum.1
  86.2 19.8 %collective-permute-start.10 = (bf16[1024,512]{1,0:T(8,128)(2,1)S(1)}, bf16[1024,512]{1,0:T(8,128)(2,1)S(1)}, u32[]{:S(2)}, u32[]{:S(2)}) collective-permute-start(bf16[1024,512]{1,0:T(8,128)(2,1)S(1)} %far_sum.1), channel_id=1, source_target_pairs={{0,8},{2,10},{4,12},{6,14},{9,1},{11,3},{13,5},{15,7},{16,24},{18,... | collective-permute-start | bytes 3145736 | tf_op jit(solution)/shard_map/ppermute | solution.py:395
  106.1 2.0 %collective-permute-start.11 = (bf16[4,512,128]{2,1,0:T(8,128)(2,1)S(1)}, bf16[4,512,128]{2,1,0:T(8,128)(2,1)S(1)}, u32[]{:S(2)}, u32[]{:S(2)}) collective-permute-start(bf16[4,512,128]{2,1,0:T(8,128)(2,1)S(1)} %get-tuple-element.33.dep_ref), channel_id=1, source_target_pairs={{0,2},{1,3},{2,0},{3,1},{4,6},{5,7},{6,4},{7,5},{8,10},{9,11},{10,... | collective-permute-start | bytes 1572872 | tf_op jit(solution)/shard_map/ppermute | solution.py:398
  108.1 7.2 %collective-permute-done.12.got_ref = bf16[4,512,128]{2,1,0:T(8,128)(2,1)S(1)} collective-permute-done((bf16[4,512,128]{2,1,0:T(8,128)(2,1)S(1)}, bf16[4,512,128]{2,1,0:T(8,128)(2,1)S(1)}, u32[]{:S(2)}, u32[]{:S(2)}) %collective-permute-start.12) | collective-permute-done | bytes 524320 | tf_op jit(solution)/shard_map/ppermute | solution.py:398
  115.2 3.2 %collective-permute-done.10.dep_ref.back_ref = bf16[1024,512]{1,0:T(8,128)(2,1)S(1)} collective-permute-done((bf16[1024,512]{1,0:T(8,128)(2,1)S(1)}, bf16[1024,512]{1,0:T(8,128)(2,1)S(1)}, u32[]{:S(2)}, u32[]{:S(2)}) %collective-permute-start.10) | collective-permute-done | bytes 1048608 | tf_op jit(solution)/shard_map/ppermute | solution.py:395
  118.5 0.6 fold.8
  119.2 1.7 %collective-permute-done.11.got_ref = bf16[4,512,128]{2,1,0:T(8,128)(2,1)S(1)} collective-permute-done((bf16[4,512,128]{2,1,0:T(8,128)(2,1)S(1)}, bf16[4,512,128]{2,1,0:T(8,128)(2,1)S(1)}, u32[]{:S(2)}, u32[]{:S(2)}) %collective-permute-start.11) | collective-permute-done | bytes 524320 | tf_op jit(solution)/shard_map/ppermute | solution.py:398
  120.9 0.7 fold.9
  122.0 6.5 %collective-permute-done.14.got_ref = bf16[2,512,128]{2,1,0:T(8,128)(2,1)S(1)} collective-permute-done((bf16[2,512,128]{2,1,0:T(8,128)(2,1)S(1)}, bf16[2,512,128]{2,1,0:T(8,128)(2,1)S(1)}, u32[]{:S(2)}, u32[]{:S(2)}) %collective-permute-start.14) | collective-permute-done | bytes 262176 | tf_op jit(solution)/shard_map/ppermute | solution.py:398
  128.4 0.6 fold.10
  129.0 2.3 %collective-permute-done.13.got_ref = bf16[2,512,128]{2,1,0:T(8,128)(2,1)S(1)} collective-permute-done((bf16[2,512,128]{2,1,0:T(8,128)(2,1)S(1)}, bf16[2,512,128]{2,1,0:T(8,128)(2,1)S(1)}, u32[]{:S(2)}, u32[]{:S(2)}) %collective-permute-start.13) | collective-permute-done | bytes 262176 | tf_op jit(solution)/shard_map/ppermute | solution.py:398
  131.3 0.6 fold.11
  131.9 6.6 %collective-permute-start.16 = (bf16[1,512,128]{2,1,0:T(8,128)(2,1)S(1)}, bf16[1,512,128]{2,1,0:T(8,128)(2,1)S(1)}, u32[]{:S(2)}, u32[]{:S(2)}) collective-permute-start(bf16[1,512,128]{2,1,0:T(8,128)(2,1)S(1)} %get-tuple-element.41.dep_ref), channel_id=1, source_target_pairs={{0,8},{1,9},{2,10},{3,11},{4,12},{5,13},{6,14},{7,15},{8,0},{9,1},... | collective-permute-start | bytes 393224 | tf_op jit(solution)/shard_map/ppermute | solution.py:398
  138.6 2.2 %grad_table.1 = f32[1024,512]{1,0:T(8,128)} custom-call(s32[7]{0:T(128)S(1)} %stack.23.info_ref, f32[1024,512]{1,0:T(8,128)S(1)} %tables.3.dep_ref.acc_ref, f32[1024,512]{1,0:T(8,128)S(1)} %collective-permute-done.6.near_ref, bf16[1024,512]{1,0:T(8,128)(2,1)S(1)} %collective-permute-done.10.dep_ref.back_ref, bf16[1,512,128]{2,1,0:T(8,128)(2,1)S(1)} %get-tuple-element.41.dep_ref), custom_call_target="tpu_custom_call" | custom-call | tf_op jit(solution)/shard_map/grad_table/pallas_call | solution.py:400
  140.7 6.0 %collective-permute-done.16.refs_1_ = bf16[1,512,128]{2,1,0:T(8,128)(2,1)S(1)} collective-permute-done((bf16[1,512,128]{2,1,0:T(8,128)(2,1)S(1)}, bf16[1,512,128]{2,1,0:T(8,128)(2,1)S(1)}, u32[]{:S(2)}, u32[]{:S(2)}) %collective-permute-start.16) | collective-permute-done | bytes 131104 | tf_op jit(solution)/shard_map/ppermute | solution.py:398
  146.7 1.7 %collective-permute-done.15.refs_0_ = bf16[1,512,128]{2,1,0:T(8,128)(2,1)S(1)} collective-permute-done((bf16[1,512,128]{2,1,0:T(8,128)(2,1)S(1)}, bf16[1,512,128]{2,1,0:T(8,128)(2,1)S(1)}, u32[]{:S(2)}, u32[]{:S(2)}) %collective-permute-start.15) | collective-permute-done | bytes 131104 | tf_op jit(solution)/shard_map/ppermute | solution.py:398
  148.4 0.9 grad_relation.1
  (31 shorter events, 1.7 us)
Async XLA Ops:
  1.3 0.8 copy-start.6
  2.0 0.7 copy-start.7
  2.8 0.7 copy-start.8
  3.5 0.7 copy-start.9
  4.3 2.0 %collective-permute-start.2 = (s32[16,1280]{1,0:T(8,128)S(1)}, s32[16,1280]{1,0:T(8,128)S(1)}, u32[]{:S(2)}, u32[]{:S(2)}) collective-permute-start(s32[16,1280]{1,0:T(8,128)S(1)} %pack.1), channel_id=1, source_target_pairs={{8,1},{10,3},{12,5},{14,7},{1,8},{3,10},{5,12},{7,14},{24,17},{26,... | collective-permute-start | bytes 245768 | tf_op jit(solution)/shard_map/ppermute | solution.py:295
  5.0 9.0 %collective-permute-start.1 = (s32[16,1280]{1,0:T(8,128)S(1)}, s32[16,1280]{1,0:T(8,128)S(1)}, u32[]{:S(2)}, u32[]{:S(2)}) collective-permute-start(s32[16,1280]{1,0:T(8,128)S(1)} %pack.1), channel_id=1, source_target_pairs={{8,0},{10,2},{12,4},{14,6},{1,9},{3,11},{5,13},{7,15},{24,16},{26,... | collective-permute-start | bytes 245768 | tf_op jit(solution)/shard_map/ppermute | solution.py:295
  15.3 28.4 %collective-permute-start.3 = (bf16[1024,512]{1,0:T(8,128)(2,1)S(1)}, bf16[1024,512]{1,0:T(8,128)(2,1)S(1)}, u32[]{:S(2)}, u32[]{:S(2)}) collective-permute-start(bf16[1024,512]{1,0:T(8,128)(2,1)S(1)} %relay.1), channel_id=1, source_target_pairs={{8,0},{10,2},{12,4},{14,6},{1,9},{3,11},{5,13},{7,15},{24,16},{26,... | collective-permute-start | bytes 3145736 | tf_op jit(solution)/shard_map/ppermute | solution.py:305
  16.6 5.8 %collective-permute-start = (s32[16,1280]{1,0:T(8,128)S(1)}, s32[16,1280]{1,0:T(8,128)S(1)}, u32[]{:S(2)}, u32[]{:S(2)}) collective-permute-start(s32[16,1280]{1,0:T(8,128)S(1)} %pack.1), channel_id=1, source_target_pairs={{0,1},{2,3},{4,5},{6,7},{9,8},{11,10},{13,12},{15,14},{16,17},{18,... | collective-permute-start | bytes 245768 | tf_op jit(solution)/shard_map/ppermute | solution.py:293
  19.6 26.4 %collective-permute-start.4 = (bf16[1024,512]{1,0:T(8,128)(2,1)}, bf16[1024,512]{1,0:T(8,128)(2,1)}, u32[]{:S(2)}, u32[]{:S(2)}) collective-permute-start(bf16[1024,512]{1,0:T(8,128)(2,1)} %table_ref.3), channel_id=1, source_target_pairs={{0,1},{2,3},{4,5},{6,7},{9,8},{11,10},{13,12},{15,14},{16,17},{18,... | collective-permute-start | bytes 3145736 | tf_op jit(solution)/shard_map/ppermute | solution.py:323
  24.5 3.4 %copy-start = (f32[4096,512]{1,0:T(8,128)S(1)}, f32[4096,512]{1,0:T(8,128)}, u32[]{:S(2)}) copy-start(f32[4096,512]{1,0:T(8,128)} %table_ref.2) | copy-start | bytes 25165828
  33.0 2.6 %copy-start.1 = (f32[12,256,512]{2,1,0:T(8,128)}, f32[12,256,512]{2,1,0:T(8,128)S(1)}, u32[]{:S(2)}) copy-start(f32[12,256,512]{2,1,0:T(8,128)S(1)} %get-tuple-element.23.rel_rows_ref) | copy-start | bytes 18874372
  35.6 0.6 copy-start.4
  43.6 1.0 copy-start.2
  43.6 4.7 %copy-start.5 = (f32[12,1,1024]{2,1,0:T(1,128)S(1)}, f32[12,1,1024]{2,1,0:T(1,128)}, u32[]{:S(2)}) copy-start(f32[12,1,1024]{2,1,0:T(1,128)} %copy-done.4) | copy-start | bytes 147460
  44.6 3.8 %collective-permute-start.5 = (bf16[1024,512]{1,0:T(8,128)(2,1)}, bf16[1024,512]{1,0:T(8,128)(2,1)S(1)}, u32[]{:S(2)}, u32[]{:S(2)}) collective-permute-start(bf16[1024,512]{1,0:T(8,128)(2,1)} %tie.1.far_ref), channel_id=1, source_target_pairs={{0,1},{2,3},{4,5},{6,7},{9,8},{11,10},{13,12},{15,14},{16,17},{18,... | collective-permute-start | bytes 3145736 | tf_op jit(solution)/shard_map/ppermute | solution.py:324
  48.4 1.2 copy-start.3
  75.5 9.8 %collective-permute-start.7 = (f32[1024,512]{1,0:T(8,128)S(1)}, f32[1024,512]{1,0:T(8,128)S(1)}, u32[]{:S(2)}, u32[]{:S(2)}) collective-permute-start(f32[1024,512]{1,0:T(8,128)S(1)} %tables.2.dep_ref.acc_ref), channel_id=1, source_target_pairs={{1,0},{3,2},{5,4},{7,6},{8,9},{10,11},{12,13},{14,15},{17,16},{19,... | collective-permute-start | bytes 6291464 | tf_op jit(solution)/shard_map/ppermute | solution.py:365
  76.8 6.5 %collective-permute-start.9 = (bf16[8,512,128]{2,1,0:T(8,128)(2,1)S(1)}, bf16[8,512,128]{2,1,0:T(8,128)(2,1)S(1)}, u32[]{:S(2)}, u32[]{:S(2)}) collective-permute-start(bf16[8,512,128]{2,1,0:T(8,128)(2,1)S(1)} %get-tuple-element.30), channel_id=1, source_target_pairs={{0,1},{1,0},{2,3},{3,2},{4,5},{5,4},{6,7},{7,6},{8,9},{9,8},{10,11... | collective-permute-start | bytes 3145736 | tf_op jit(solution)/shard_map/ppermute | solution.py:371
  78.1 6.4 %collective-permute-start.8 = (bf16[8,512,128]{2,1,0:T(8,128)(2,1)S(1)}, bf16[8,512,128]{2,1,0:T(8,128)(2,1)S(1)}, u32[]{:S(2)}, u32[]{:S(2)}) collective-permute-start(bf16[8,512,128]{2,1,0:T(8,128)(2,1)S(1)} %get-tuple-element.28), channel_id=1, source_target_pairs={{0,1},{1,0},{2,3},{3,2},{4,5},{5,4},{6,7},{7,6},{8,9},{9,8},{10,11... | collective-permute-start | bytes 3145736 | tf_op jit(solution)/shard_map/ppermute | solution.py:371
  82.0 56.6 %collective-permute-start.6 = (f32[1024,512]{1,0:T(8,128)S(1)}, f32[1024,512]{1,0:T(8,128)S(1)}, u32[]{:S(2)}, u32[]{:S(2)}) collective-permute-start(f32[1024,512]{1,0:T(8,128)S(1)} %tables.3.dep_ref.acc_ref), channel_id=1, source_target_pairs={{1,0},{3,2},{5,4},{7,6},{8,9},{10,11},{12,13},{14,15},{17,16},{19,... | collective-permute-start | bytes 6291464 | tf_op jit(solution)/shard_map/ppermute | solution.py:368
  86.2 32.3 %collective-permute-start.10 = (bf16[1024,512]{1,0:T(8,128)(2,1)S(1)}, bf16[1024,512]{1,0:T(8,128)(2,1)S(1)}, u32[]{:S(2)}, u32[]{:S(2)}) collective-permute-start(bf16[1024,512]{1,0:T(8,128)(2,1)S(1)} %far_sum.1), channel_id=1, source_target_pairs={{0,8},{2,10},{4,12},{6,14},{9,1},{11,3},{13,5},{15,7},{16,24},{18,... | collective-permute-start | bytes 3145736 | tf_op jit(solution)/shard_map/ppermute | solution.py:395
  106.0 9.2 %collective-permute-start.12 = (bf16[4,512,128]{2,1,0:T(8,128)(2,1)S(1)}, bf16[4,512,128]{2,1,0:T(8,128)(2,1)S(1)}, u32[]{:S(2)}, u32[]{:S(2)}) collective-permute-start(bf16[4,512,128]{2,1,0:T(8,128)(2,1)S(1)} %get-tuple-element.32.dep_ref), channel_id=1, source_target_pairs={{0,2},{1,3},{2,0},{3,1},{4,6},{5,7},{6,4},{7,5},{8,10},{9,11},{10,... | collective-permute-start | bytes 1572872 | tf_op jit(solution)/shard_map/ppermute | solution.py:398
  106.1 14.8 %collective-permute-start.11 = (bf16[4,512,128]{2,1,0:T(8,128)(2,1)S(1)}, bf16[4,512,128]{2,1,0:T(8,128)(2,1)S(1)}, u32[]{:S(2)}, u32[]{:S(2)}) collective-permute-start(bf16[4,512,128]{2,1,0:T(8,128)(2,1)S(1)} %get-tuple-element.33.dep_ref), channel_id=1, source_target_pairs={{0,2},{1,3},{2,0},{3,1},{4,6},{5,7},{6,4},{7,5},{8,10},{9,11},{10,... | collective-permute-start | bytes 1572872 | tf_op jit(solution)/shard_map/ppermute | solution.py:398
  119.1 9.3 %collective-permute-start.14 = (bf16[2,512,128]{2,1,0:T(8,128)(2,1)S(1)}, bf16[2,512,128]{2,1,0:T(8,128)(2,1)S(1)}, u32[]{:S(2)}, u32[]{:S(2)}) collective-permute-start(bf16[2,512,128]{2,1,0:T(8,128)(2,1)S(1)} %get-tuple-element.36.dep_ref), channel_id=1, source_target_pairs={{0,4},{1,5},{2,6},{3,7},{4,0},{5,1},{6,2},{7,3},{8,12},{9,13},{10,... | collective-permute-start | bytes 786440 | tf_op jit(solution)/shard_map/ppermute | solution.py:398
  121.5 9.8 %collective-permute-start.13 = (bf16[2,512,128]{2,1,0:T(8,128)(2,1)S(1)}, bf16[2,512,128]{2,1,0:T(8,128)(2,1)S(1)}, u32[]{:S(2)}, u32[]{:S(2)}) collective-permute-start(bf16[2,512,128]{2,1,0:T(8,128)(2,1)S(1)} %get-tuple-element.37.dep_ref), channel_id=1, source_target_pairs={{0,4},{1,5},{2,6},{3,7},{4,0},{5,1},{6,2},{7,3},{8,12},{9,13},{10,... | collective-permute-start | bytes 786440 | tf_op jit(solution)/shard_map/ppermute | solution.py:398
  131.9 14.8 %collective-permute-start.16 = (bf16[1,512,128]{2,1,0:T(8,128)(2,1)S(1)}, bf16[1,512,128]{2,1,0:T(8,128)(2,1)S(1)}, u32[]{:S(2)}, u32[]{:S(2)}) collective-permute-start(bf16[1,512,128]{2,1,0:T(8,128)(2,1)S(1)} %get-tuple-element.41.dep_ref), channel_id=1, source_target_pairs={{0,8},{1,9},{2,10},{3,11},{4,12},{5,13},{6,14},{7,15},{8,0},{9,1},... | collective-permute-start | bytes 393224 | tf_op jit(solution)/shard_map/ppermute | solution.py:398
  138.5 9.9 %collective-permute-start.15 = (bf16[1,512,128]{2,1,0:T(8,128)(2,1)S(1)}, bf16[1,512,128]{2,1,0:T(8,128)(2,1)S(1)}, u32[]{:S(2)}, u32[]{:S(2)}) collective-permute-start(bf16[1,512,128]{2,1,0:T(8,128)(2,1)S(1)} %get-tuple-element.40.dep_ref), channel_id=1, source_target_pairs={{0,8},{1,9},{2,10},{3,11},{4,12},{5,13},{6,14},{7,15},{8,0},{9,1},... | collective-permute-start | bytes 393224 | tf_op jit(solution)/shard_map/ppermute | solution.py:398

commit v2 on v1

--- a/solution.py
+++ b/solution.py
@@ -246,14 +246,15 @@
             ]
 
 
-def tie(x, dep):
+def relay(x, dep):
     return pl.pallas_call(
-        lambda x_ref, dep_ref, out_ref: None,
+        relay_kernel,
         out_shape=jax.ShapeDtypeStruct(x.shape, x.dtype),
         in_specs=[ANY, ANY],
-        out_specs=ANY,
-        input_output_aliases={0: 0},
-        name="tie",
+        out_specs=VMEM,
+        scratch_shapes=[pltpu.SemaphoreType.DMA],
+        compiler_params=params(2),
+        name="relay",
     )(x, dep)
 
 
@@ -293,15 +294,7 @@
     from_lead = lax.ppermute(mine, "ent", to_mate)
     first = jnp.where(lead, mine, from_lead)
     second = lax.ppermute(mine, "ent", cross) + lax.ppermute(mine, "ent", cross_mate)
-    sent = pl.pallas_call(
-        relay_kernel,
-        out_shape=shape(entity_table.shape, BF),
-        in_specs=[ANY, ANY],
-        out_specs=VMEM,
-        scratch_shapes=[pltpu.SemaphoreType.DMA],
-        compiler_params=params(2),
-        name="relay",
-    )(entity_table, second)
+    sent = relay(entity_table, second)
     far = lax.ppermute(sent, "ent", cross)
     ids = jnp.concatenate([first[:cap], second[:cap]], axis=0)
     bits = [(me >> b) & 1 for b in range(devices.bit_length() - 1)]
@@ -319,7 +312,7 @@
         name="prep",
     )(info, rel_ids, ids_t, relation_table)
 
-    far = tie(far, mult)
+    far = relay(far, rel_rows)
     mate_table = lax.ppermute(entity_table, "ent", to_mate)
     mate_far = lax.ppermute(far, "ent", to_mate)
 

time: 150 us -> 152 us (1.013)
  the two profiles are of different devices: /device:TPU:4 before, /device:TPU:0 now
where the time goes in v2:
time: 152 us; the launch traced here: 154 us
  waiting for transfers between devices  62.1 us (41%)
  Pallas kernels  45 us (30%)
  starting transfers between devices  36.8 us (24%)
  local copies, waits for them, and re-layouts  8.92 us (6%)
  between operations  1.62 us (1%)
    ppermute x8, waiting for transfers between devices, shards(): lax.ppermute(g, 'ent', [(i, i ^ bit) for i in range(devices)])  40.1 us
    ppermute x8, starting transfers between devices, shards(): lax.ppermute(g, 'ent', [(i, i ^ bit) for i in range(devices)])  23 us
    pallas_call x1, Pallas kernels, shards(): pl.pallas_call(functools.partial(span_kernel, cap), out_shape=(shape((cap...  21.9 us
    ppermute x1, waiting for transfers between devices, shards(): far = lax.ppermute(sent, 'ent', cross)  10.7 us
    ppermute x1, waiting for transfers between devices, shards(): lax.ppermute(mine, 'ent', cross) + lax.ppermute(mine, 'ent', cross_mate)  9.14 us
    pallas_call x2, Pallas kernels, table_side(): pl.pallas_call(functools.partial(table_kernel, cap, side), out_shape=shap...  7.83 us
    unnamed x12, local copies, waits for them, and re-layouts  6.28 us
    pallas_call x1, Pallas kernels, shards(): pl.pallas_call(functools.partial(prep_kernel, cap), out_shape=(shape((cap...  5.1 us
  transfers between devices with their start and end apart: 17, of which 9 were waited for; matrix products, arithmetic and copies ran while one was open for 2% of the time, Pallas kernels for 11%

profile of v2, /device:TPU:0, one launch (start us, length us, event | category | flops | bytes accessed | tf_op | source)
XLA Modules:
  0.0 154.5 jit_solution(12696706004084351052)
XLA Ops:
  1.3 0.7 copy-done.2
  2.0 0.7 copy-done.3
  2.8 0.7 copy-done.4
  3.5 0.7 copy-done.5
  4.2 0.1 pack.1
  4.3 0.7 collective-permute-start.2
  5.0 1.3 collective-permute-start.1
  6.3 9.1 %collective-permute-done.1 = s32[16,1280]{1,0:T(8,128)S(1)} collective-permute-done((s32[16,1280]{1,0:T(8,128)S(1)}, s32[16,1280]{1,0:T(8,128)S(1)}, u32[]{:S(2)}, u32[]{:S(2)}) %collective-permute-start.1) | collective-permute-done | bytes 81952 | tf_op jit(solution)/shard_map/ppermute | solution.py:296
  15.5 1.2 relay.2
  16.7 1.3 collective-permute-start.3
  18.0 3.9 %collective-permute-start = (s32[16,1280]{1,0:T(8,128)S(1)}, s32[16,1280]{1,0:T(8,128)S(1)}, u32[]{:S(2)}, u32[]{:S(2)}) collective-permute-start(s32[16,1280]{1,0:T(8,128)S(1)} %pack.1), channel_id=1, source_target_pairs={{0,1},{2,3},{4,5},{6,7},{9,8},{11,10},{13,12},{15,14},{16,17},{18,... | collective-permute-start | bytes 245768 | tf_op jit(solution)/shard_map/ppermute | solution.py:294
  21.9 1.4 collective-permute-start.4
  23.3 0.5 slice.21
  23.8 0.5 slice.20
  24.4 0.2 copy.10.ids_t_ref
  24.6 1.4 stack.23.info_ref
  26.0 3.4 %copy-done.1 = f32[4096,512]{1,0:T(8,128)S(1)} copy-done((f32[4096,512]{1,0:T(8,128)S(1)}, f32[4096,512]{1,0:T(8,128)}, u32[]{:S(2)}) %copy-start.1) | copy-done | bytes 8388632
  29.4 5.1 %prep.1 = (f32[12,256,512]{2,1,0:T(8,128)S(1)}, f32[12,1,1024]{2,1,0:T(1,128)S(1)}) custom-call(s32[7]{0:T(128)S(1)} %stack.23.info_ref, s32[24,256]{1,0:T(8,128)S(1)} %fusion.rel_ids_ref, s32[1280,24]{1,0:T(8,128)S(1)} %copy.10.ids_t_ref, f32[4096,512]{1,0:T(8,128)S(1)} %copy-done.1), custom_call_target="tpu_custom_call" | custom-call | flops 1 | bytes 1 | tf_op jit(solution)/shard_map/prep/pallas_call | solution.py:305
  34.5 10.7 %collective-permute-done.3.x_ref = bf16[1024,512]{1,0:T(8,128)(2,1)} collective-permute-done((bf16[1024,512]{1,0:T(8,128)(2,1)S(1)}, bf16[1024,512]{1,0:T(8,128)(2,1)}, u32[]{:S(2)}, u32[]{:S(2)}) %collective-permute-start.3) | collective-permute-done | bytes 1048608 | tf_op jit(solution)/shard_map/ppermute | solution.py:298
  45.2 1.2 relay.3.far_ref
  46.4 1.4 collective-permute-start.5
  47.8 2.2 %collective-permute-done.5.mate_far_ref = bf16[1024,512]{1,0:T(8,128)(2,1)S(1)} collective-permute-done((bf16[1024,512]{1,0:T(8,128)(2,1)S(1)}, bf16[1024,512]{1,0:T(8,128)(2,1)S(1)}, u32[]{:S(2)}, u32[]{:S(2)}) %collective-permute-start.5) | collective-permute-done | bytes 1048608 | tf_op jit(solution)/shard_map/ppermute | solution.py:317
  50.0 21.9 %spans.1 = (bf16[12,256,1024]{2,1,0:T(8,128)(2,1)S(1)}, bf16[12,256,512]{2,1,0:T(8,128)(2,1)S(1)}, bf16[12,256,512]{2,1,0:T(8,128)(2,1)S(1)}, f32[8,512,128]{2,1...) custom-call(s32[7]{0:T(128)S(1)} %stack.23.info_ref, ...), custom_call_target="tpu_custom_call" | custom-call | tf_op jit(solution)/shard_map/spans/pallas_call | solution.py:320
  71.9 4.0 %tables.2.dep_ref.acc_ref = f32[1024,512]{1,0:T(8,128)S(1)} custom-call(s32[7]{0:T(128)S(1)} %stack.23.info_ref, s32[24,1280]{1,0:T(8,128)S(1)} %pad_add_fusion.ids_ref, bf16[12,256,1024]{2,1,0:T(8,128)(2,1)S(1)} %get-tuple-element.25.mixed_ref.dep_ref, bf16[12,256,512]{2,1,0:T(8,128)(2,1)S(1)} %get-tuple-element.26.scaled_ref, ...), custom_call_target="tpu_custom_call" | custom-call | flops 3221225472 | bytes 12582912 | tf_op jit(solution)/shard_map/tables/pallas_call | solution.py:345
  75.8 1.3 collective-permute-start.7
  77.2 1.3 collective-permute-start.9
  78.5 0.1 collective-permute-start.8
  78.6 3.9 %tables.3.dep_ref.acc_ref = f32[1024,512]{1,0:T(8,128)S(1)} custom-call(s32[7]{0:T(128)S(1)} %stack.23.info_ref, s32[24,1280]{1,0:T(8,128)S(1)} %pad_add_fusion.ids_ref, bf16[12,256,1024]{2,1,0:T(8,128)(2,1)S(1)} %get-tuple-element.25.mixed_ref.dep_ref, bf16[12,256,512]{2,1,0:T(8,128)(2,1)S(1)} %get-tuple-element.26.scaled_ref, ...), custom_call_target="tpu_custom_call" | custom-call | flops 3221225472 | bytes 12582912 | tf_op jit(solution)/shard_map/tables/pallas_call | solution.py:345
  82.4 1.3 collective-permute-start.6
  83.7 0.7 fold.6
  84.4 0.5 collective-permute-done.8.got_ref
  84.9 0.7 fold.7
  85.6 0.7 far_sum.1
  86.4 1.4 collective-permute-start.10
  87.7 18.4 %collective-permute-start.12 = (bf16[4,512,128]{2,1,0:T(8,128)(2,1)S(1)}, bf16[4,512,128]{2,1,0:T(8,128)(2,1)S(1)}, u32[]{:S(2)}, u32[]{:S(2)}) collective-permute-start(bf16[4,512,128]{2,1,0:T(8,128)(2,1)S(1)} %get-tuple-element.32.dep_ref), channel_id=1, source_target_pairs={{0,2},{1,3},{2,0},{3,1},{4,6},{5,7},{6,4},{7,5},{8,10},{9,11},{10,... | collective-permute-start | bytes 1572872 | tf_op jit(solution)/shard_map/ppermute | solution.py:391
  106.1 0.1 collective-permute-start.11
  106.2 12.4 %collective-permute-done.12.got_ref = bf16[4,512,128]{2,1,0:T(8,128)(2,1)S(1)} collective-permute-done((bf16[4,512,128]{2,1,0:T(8,128)(2,1)S(1)}, bf16[4,512,128]{2,1,0:T(8,128)(2,1)S(1)}, u32[]{:S(2)}, u32[]{:S(2)}) %collective-permute-start.12) | collective-permute-done | bytes 524320 | tf_op jit(solution)/shard_map/ppermute | solution.py:391
  118.6 0.6 fold.8
  119.3 10.5 %collective-permute-done.11.got_ref = bf16[4,512,128]{2,1,0:T(8,128)(2,1)S(1)} collective-permute-done((bf16[4,512,128]{2,1,0:T(8,128)(2,1)S(1)}, bf16[4,512,128]{2,1,0:T(8,128)(2,1)S(1)}, u32[]{:S(2)}, u32[]{:S(2)}) %collective-permute-start.11) | collective-permute-done | bytes 524320 | tf_op jit(solution)/shard_map/ppermute | solution.py:391
  129.8 0.6 fold.9
  130.5 0.6 fold.10
  131.1 7.7 %collective-permute-done.13.got_ref = bf16[2,512,128]{2,1,0:T(8,128)(2,1)S(1)} collective-permute-done((bf16[2,512,128]{2,1,0:T(8,128)(2,1)S(1)}, bf16[2,512,128]{2,1,0:T(8,128)(2,1)S(1)}, u32[]{:S(2)}, u32[]{:S(2)}) %collective-permute-start.13) | collective-permute-done | bytes 262176 | tf_op jit(solution)/shard_map/ppermute | solution.py:391
  138.9 0.6 fold.11
  139.5 2.9 %collective-permute-start.15 = (bf16[1,512,128]{2,1,0:T(8,128)(2,1)S(1)}, bf16[1,512,128]{2,1,0:T(8,128)(2,1)S(1)}, u32[]{:S(2)}, u32[]{:S(2)}) collective-permute-start(bf16[1,512,128]{2,1,0:T(8,128)(2,1)S(1)} %get-tuple-element.40.dep_ref), channel_id=1, source_target_pairs={{0,8},{1,9},{2,10},{3,11},{4,12},{5,13},{6,14},{7,15},{8,0},{9,1},... | collective-permute-start | bytes 393224 | tf_op jit(solution)/shard_map/ppermute | solution.py:391
  142.4 2.1 %grad_table.1 = f32[1024,512]{1,0:T(8,128)} custom-call(s32[7]{0:T(128)S(1)} %stack.23.info_ref, f32[1024,512]{1,0:T(8,128)S(1)} %tables.3.dep_ref.acc_ref, f32[1024,512]{1,0:T(8,128)S(1)} %collective-permute-done.6.near_ref, bf16[1024,512]{1,0:T(8,128)(2,1)S(1)} %collective-permute-done.10.dep_ref.back_ref, bf16[1,512,128]{2,1,0:T(8,128)(2,1)S(1)} %get-tuple-element.41.dep_ref), custom_call_target="tpu_custom_call" | custom-call | tf_op jit(solution)/shard_map/grad_table/pallas_call | solution.py:393
  144.6 6.3 %collective-permute-done.16.refs_1_ = bf16[1,512,128]{2,1,0:T(8,128)(2,1)S(1)} collective-permute-done((bf16[1,512,128]{2,1,0:T(8,128)(2,1)S(1)}, bf16[1,512,128]{2,1,0:T(8,128)(2,1)S(1)}, u32[]{:S(2)}, u32[]{:S(2)}) %collective-permute-start.16) | collective-permute-done | bytes 131104 | tf_op jit(solution)/shard_map/ppermute | solution.py:391
  150.9 2.7 %collective-permute-done.15.refs_0_ = bf16[1,512,128]{2,1,0:T(8,128)(2,1)S(1)} collective-permute-done((bf16[1,512,128]{2,1,0:T(8,128)(2,1)S(1)}, bf16[1,512,128]{2,1,0:T(8,128)(2,1)S(1)}, u32[]{:S(2)}, u32[]{:S(2)}) %collective-permute-start.15) | collective-permute-done | bytes 131104 | tf_op jit(solution)/shard_map/ppermute | solution.py:391
  153.6 0.9 grad_relation.1
  (23 shorter events, 0.3 us)
Async XLA Ops:
  1.3 0.8 copy-start.2
  2.0 0.7 copy-start.3
  2.8 0.7 copy-start.4
  3.5 0.7 copy-start.5
  4.3 2.0 %collective-permute-start.2 = (s32[16,1280]{1,0:T(8,128)S(1)}, s32[16,1280]{1,0:T(8,128)S(1)}, u32[]{:S(2)}, u32[]{:S(2)}) collective-permute-start(s32[16,1280]{1,0:T(8,128)S(1)} %pack.1), channel_id=1, source_target_pairs={{8,1},{10,3},{12,5},{14,7},{1,8},{3,10},{5,12},{7,14},{24,17},{26,... | collective-permute-start | bytes 245768 | tf_op jit(solution)/shard_map/ppermute | solution.py:296
  5.0 10.5 %collective-permute-start.1 = (s32[16,1280]{1,0:T(8,128)S(1)}, s32[16,1280]{1,0:T(8,128)S(1)}, u32[]{:S(2)}, u32[]{:S(2)}) collective-permute-start(s32[16,1280]{1,0:T(8,128)S(1)} %pack.1), channel_id=1, source_target_pairs={{8,0},{10,2},{12,4},{14,6},{1,9},{3,11},{5,13},{7,15},{24,16},{26,... | collective-permute-start | bytes 245768 | tf_op jit(solution)/shard_map/ppermute | solution.py:296
  16.7 28.5 %collective-permute-start.3 = (bf16[1024,512]{1,0:T(8,128)(2,1)S(1)}, bf16[1024,512]{1,0:T(8,128)(2,1)}, u32[]{:S(2)}, u32[]{:S(2)}) collective-permute-start(bf16[1024,512]{1,0:T(8,128)(2,1)S(1)} %relay.2), channel_id=1, source_target_pairs={{8,0},{10,2},{12,4},{14,6},{1,9},{3,11},{5,13},{7,15},{24,16},{26,... | collective-permute-start | bytes 3145736 | tf_op jit(solution)/shard_map/ppermute | solution.py:298
  18.0 5.8 %collective-permute-start = (s32[16,1280]{1,0:T(8,128)S(1)}, s32[16,1280]{1,0:T(8,128)S(1)}, u32[]{:S(2)}, u32[]{:S(2)}) collective-permute-start(s32[16,1280]{1,0:T(8,128)S(1)} %pack.1), channel_id=1, source_target_pairs={{0,1},{2,3},{4,5},{6,7},{9,8},{11,10},{13,12},{15,14},{16,17},{18,... | collective-permute-start | bytes 245768 | tf_op jit(solution)/shard_map/ppermute | solution.py:294
  21.9 25.9 %collective-permute-start.4 = (bf16[1024,512]{1,0:T(8,128)(2,1)}, bf16[1024,512]{1,0:T(8,128)(2,1)S(1)}, u32[]{:S(2)}, u32[]{:S(2)}) collective-permute-start(bf16[1024,512]{1,0:T(8,128)(2,1)} %table_ref.3), channel_id=1, source_target_pairs={{0,1},{2,3},{4,5},{6,7},{9,8},{11,10},{13,12},{15,14},{16,17},{18,... | collective-permute-start | bytes 3145736 | tf_op jit(solution)/shard_map/ppermute | solution.py:316
  26.0 3.4 %copy-start.1 = (f32[4096,512]{1,0:T(8,128)S(1)}, f32[4096,512]{1,0:T(8,128)}, u32[]{:S(2)}) copy-start(f32[4096,512]{1,0:T(8,128)} %table_ref.2) | copy-start | bytes 25165828
  34.5 12.0 %copy-start = (f32[12,256,512]{2,1,0:T(8,128)}, f32[12,256,512]{2,1,0:T(8,128)S(1)}, u32[]{:S(2)}) copy-start(f32[12,256,512]{2,1,0:T(8,128)S(1)} %get-tuple-element.23.dep_ref.rel_rows_ref) | copy-start | bytes 18874372
  46.4 3.6 %collective-permute-start.5 = (bf16[1024,512]{1,0:T(8,128)(2,1)S(1)}, bf16[1024,512]{1,0:T(8,128)(2,1)S(1)}, u32[]{:S(2)}, u32[]{:S(2)}) collective-permute-start(bf16[1024,512]{1,0:T(8,128)(2,1)S(1)} %relay.3.far_ref), channel_id=1, source_target_pairs={{0,1},{2,3},{4,5},{6,7},{9,8},{11,10},{13,12},{15,14},{16,17},{18,... | collective-permute-start | bytes 3145736 | tf_op jit(solution)/shard_map/ppermute | solution.py:317
  75.8 9.8 %collective-permute-start.7 = (f32[1024,512]{1,0:T(8,128)S(1)}, f32[1024,512]{1,0:T(8,128)S(1)}, u32[]{:S(2)}, u32[]{:S(2)}) collective-permute-start(f32[1024,512]{1,0:T(8,128)S(1)} %tables.2.dep_ref.acc_ref), channel_id=1, source_target_pairs={{1,0},{3,2},{5,4},{7,6},{8,9},{10,11},{12,13},{14,15},{17,16},{19,... | collective-permute-start | bytes 6291464 | tf_op jit(solution)/shard_map/ppermute | solution.py:358
  77.2 6.6 %collective-permute-start.9 = (bf16[8,512,128]{2,1,0:T(8,128)(2,1)S(1)}, bf16[8,512,128]{2,1,0:T(8,128)(2,1)S(1)}, u32[]{:S(2)}, u32[]{:S(2)}) collective-permute-start(bf16[8,512,128]{2,1,0:T(8,128)(2,1)S(1)} %get-tuple-element.30), channel_id=1, source_target_pairs={{0,1},{1,0},{2,3},{3,2},{4,5},{5,4},{6,7},{7,6},{8,9},{9,8},{10,11... | collective-permute-start | bytes 3145736 | tf_op jit(solution)/shard_map/ppermute | solution.py:364
  78.5 6.4 %collective-permute-start.8 = (bf16[8,512,128]{2,1,0:T(8,128)(2,1)S(1)}, bf16[8,512,128]{2,1,0:T(8,128)(2,1)S(1)}, u32[]{:S(2)}, u32[]{:S(2)}) collective-permute-start(bf16[8,512,128]{2,1,0:T(8,128)(2,1)S(1)} %get-tuple-element.28), channel_id=1, source_target_pairs={{0,1},{1,0},{2,3},{3,2},{4,5},{5,4},{6,7},{7,6},{8,9},{9,8},{10,11... | collective-permute-start | bytes 3145736 | tf_op jit(solution)/shard_map/ppermute | solution.py:364
  82.4 60.0 %collective-permute-start.6 = (f32[1024,512]{1,0:T(8,128)S(1)}, f32[1024,512]{1,0:T(8,128)S(1)}, u32[]{:S(2)}, u32[]{:S(2)}) collective-permute-start(f32[1024,512]{1,0:T(8,128)S(1)} %tables.3.dep_ref.acc_ref), channel_id=1, source_target_pairs={{1,0},{3,2},{5,4},{7,6},{8,9},{10,11},{12,13},{14,15},{17,16},{19,... | collective-permute-start | bytes 6291464 | tf_op jit(solution)/shard_map/ppermute | solution.py:361
  86.4 32.2 %collective-permute-start.10 = (bf16[1024,512]{1,0:T(8,128)(2,1)S(1)}, bf16[1024,512]{1,0:T(8,128)(2,1)S(1)}, u32[]{:S(2)}, u32[]{:S(2)}) collective-permute-start(bf16[1024,512]{1,0:T(8,128)(2,1)S(1)} %far_sum.1), channel_id=1, source_target_pairs={{0,8},{2,10},{4,12},{6,14},{9,1},{11,3},{13,5},{15,7},{16,24},{18,... | collective-permute-start | bytes 3145736 | tf_op jit(solution)/shard_map/ppermute | solution.py:388
  87.7 30.8 %collective-permute-start.12 = (bf16[4,512,128]{2,1,0:T(8,128)(2,1)S(1)}, bf16[4,512,128]{2,1,0:T(8,128)(2,1)S(1)}, u32[]{:S(2)}, u32[]{:S(2)}) collective-permute-start(bf16[4,512,128]{2,1,0:T(8,128)(2,1)S(1)} %get-tuple-element.32.dep_ref), channel_id=1, source_target_pairs={{0,2},{1,3},{2,0},{3,1},{4,6},{5,7},{6,4},{7,5},{8,10},{9,11},{10,... | collective-permute-start | bytes 1572872 | tf_op jit(solution)/shard_map/ppermute | solution.py:391
  106.1 23.7 %collective-permute-start.11 = (bf16[4,512,128]{2,1,0:T(8,128)(2,1)S(1)}, bf16[4,512,128]{2,1,0:T(8,128)(2,1)S(1)}, u32[]{:S(2)}, u32[]{:S(2)}) collective-permute-start(bf16[4,512,128]{2,1,0:T(8,128)(2,1)S(1)} %get-tuple-element.33.dep_ref), channel_id=1, source_target_pairs={{0,2},{1,3},{2,0},{3,1},{4,6},{5,7},{6,4},{7,5},{8,10},{9,11},{10,... | collective-permute-start | bytes 1572872 | tf_op jit(solution)/shard_map/ppermute | solution.py:391
  119.2 11.3 %collective-permute-start.14 = (bf16[2,512,128]{2,1,0:T(8,128)(2,1)S(1)}, bf16[2,512,128]{2,1,0:T(8,128)(2,1)S(1)}, u32[]{:S(2)}, u32[]{:S(2)}) collective-permute-start(bf16[2,512,128]{2,1,0:T(8,128)(2,1)S(1)} %get-tuple-element.36.dep_ref), channel_id=1, source_target_pairs={{0,4},{1,5},{2,6},{3,7},{4,0},{5,1},{6,2},{7,3},{8,12},{9,13},{10,... | collective-permute-start | bytes 786440 | tf_op jit(solution)/shard_map/ppermute | solution.py:391
  130.4 8.4 %collective-permute-start.13 = (bf16[2,512,128]{2,1,0:T(8,128)(2,1)S(1)}, bf16[2,512,128]{2,1,0:T(8,128)(2,1)S(1)}, u32[]{:S(2)}, u32[]{:S(2)}) collective-permute-start(bf16[2,512,128]{2,1,0:T(8,128)(2,1)S(1)} %get-tuple-element.37.dep_ref), channel_id=1, source_target_pairs={{0,4},{1,5},{2,6},{3,7},{4,0},{5,1},{6,2},{7,3},{8,12},{9,13},{10,... | collective-permute-start | bytes 786440 | tf_op jit(solution)/shard_map/ppermute | solution.py:391
  139.5 11.4 %collective-permute-start.16 = (bf16[1,512,128]{2,1,0:T(8,128)(2,1)S(1)}, bf16[1,512,128]{2,1,0:T(8,128)(2,1)S(1)}, u32[]{:S(2)}, u32[]{:S(2)}) collective-permute-start(bf16[1,512,128]{2,1,0:T(8,128)(2,1)S(1)} %get-tuple-element.41.dep_ref), channel_id=1, source_target_pairs={{0,8},{1,9},{2,10},{3,11},{4,12},{5,13},{6,14},{7,15},{8,0},{9,1},... | collective-permute-start | bytes 393224 | tf_op jit(solution)/shard_map/ppermute | solution.py:391
  139.5 14.0 %collective-permute-start.15 = (bf16[1,512,128]{2,1,0:T(8,128)(2,1)S(1)}, bf16[1,512,128]{2,1,0:T(8,128)(2,1)S(1)}, u32[]{:S(2)}, u32[]{:S(2)}) collective-permute-start(bf16[1,512,128]{2,1,0:T(8,128)(2,1)S(1)} %get-tuple-element.40.dep_ref), channel_id=1, source_target_pairs={{0,8},{1,9},{2,10},{3,11},{4,12},{5,13},{6,14},{7,15},{8,0},{9,1},... | collective-permute-start | bytes 393224 | tf_op jit(solution)/shard_map/ppermute | solution.py:391
